TPU v7x, 32 devices: a whole 2x2x4 slice. The times are simulated.
32 devices in a mesh: lon: 8 (over z, core), lat: 4 (over y, x).
Axes of the slice: x: 2, y: 2, z: 4, core: 2. Of those that a mesh axis runs over, the one named last changes fastest.
Arguments:
- zonal_velocity: float32 [75, 96, 3072], P(None, 'lat', 'lon'), may hold values from -6 to 6
- meridional_velocity: float32 [75, 96, 3072], P(None, 'lat', 'lon'), may hold values from -6 to 6
- tracer: float32 [75, 96, 3072], P(None, 'lat', 'lon'), may hold values from -6 to 6
- land_mask: int32 [96, 3072], P('lat', 'lon'), may hold values 0 or 1
- remap_bounds: int32 [8, 256, 31], P('lat', 'lon'), may hold values from 0 to 75, as said below
- nest_owner: int32 [8, 256], P('lat', 'lon'), may hold values from 0 to 8, as said below
Outputs:
- zonal_new: float32 [75, 96, 3072], P(None, 'lat', 'lon')
- meridional_new: float32 [75, 96, 3072], P(None, 'lat', 'lon')
- tracer_new: float32 [75, 96, 3072], P(None, 'lat', 'lon')
- nest_tiles: float32 [4, 8, 16, 30, 1296], P('lat', 'lon')
Inputs may be any that keep to these rules, and one draw needn't show every extreme that they name: `remap_bounds`: for each parent block the 31 entries rise strictly from 0 and the last lies between 30 and 75. `nest_owner`: A value below 8 puts the block in the nest, owned by the tile at that longitude index in the block's own latitude band; 8 marks a block outside the nest. Among the blocks of one tile at most 2 share an owner, and at most 16 lie in the nest.
All inputs are finite; a program needn't handle non-finite values. No bound on the sum of `land_mask` on one device may be relied on, other than what follows from the above.
Results may differ from a plain program's by a relative error of at most 0.0003.
Values sent between devices are 32-bit elements; how exact they have to be, the bound alone decides.
A program may use at most 192 MiB of HBM per device.

v0:
```python
import math

import jax
import jax.numpy as jnp
import numpy as np
from jax import lax
from jax.sharding import PartitionSpec as P

SIGMA = 30
TILE = 12
CAP = 2
BLK_X = 32
BLK_Y = 2
RIM = 256
NCELL = 1296


ADVECT = 0.25
DIFFUSE = 0.15
PRESSURE = 0.3
ROTATION = 0.6
BASE_LATITUDE = 20.0
ROW_DEGREES = 1.0 / 12.0


def padded(shard, sides, width, wrap):
    for axis, dim in sides:
        count, length = (lax.axis_size(axis), shard.shape[dim])
        up = [(i, (i + 1) % count) for i in range(count if wrap else count - 1)]
        down = [(j, i) for i, j in up]
        last = lax.slice_in_dim(shard, length - width, length, axis=dim)
        leading = lax.slice_in_dim(shard, 0, width, axis=dim)
        before = lax.ppermute(last, axis, up)
        after = lax.ppermute(leading, axis, down)
        shard = jnp.concatenate([before, shard, after], axis=dim)
    return shard


def cubic_weights(tile_cells):
    span_len = tile_cells + 4
    weights = np.zeros((span_len, 3 * tile_cells), np.float32)
    for cell_idx in range(tile_cells):
        for phase_idx in range(3):
            if phase_idx == 0:
                base_cell, fraction = (cell_idx - 1, 2.0 / 3.0)
            elif phase_idx == 1:
                base_cell, fraction = (cell_idx, 0.0)
            else:
                base_cell, fraction = (cell_idx, 1.0 / 3.0)
            coeffs = (
                (-(fraction**3) + 2 * fraction**2 - fraction) / 2,
                (3 * fraction**3 - 5 * fraction**2 + 2) / 2,
                (-3 * fraction**3 + 4 * fraction**2 + fraction) / 2,
                (fraction**3 - fraction**2) / 2,
            )
            for offset in range(4):
                weights[base_cell + 1 + offset, 3 * cell_idx + phase_idx] += coeffs[offset]
    return np.kron(weights, weights).astype(np.float32)


def coriolis_rows(row_index):
    degrees = BASE_LATITUDE + (row_index.astype(jnp.float32) + 0.5) * ROW_DEGREES
    latitude = degrees * (math.pi / 180.0)
    return (ROTATION * jnp.sin(latitude))[:, None]


def step_fields(fields, east_cell, west_cell, north_cell, south_cell, coriolis, sea_mask):
    zonal_vel = fields[0]
    merid_vel = fields[1]
    grad_x = 0.5 * (east_cell - west_cell)
    grad_y = 0.5 * (north_cell - south_cell)
    laplace = east_cell + west_cell + north_cell + south_cell - 4.0 * fields
    advect = zonal_vel[None] * grad_x + merid_vel[None] * grad_y
    zonal_out = sea_mask * (
        zonal_vel
        - ADVECT * advect[0]
        + coriolis * merid_vel
        - PRESSURE * grad_x[2]
        + DIFFUSE * laplace[0]
    )
    merid_out = sea_mask * (
        merid_vel
        - ADVECT * advect[1]
        - coriolis * zonal_vel
        - PRESSURE * grad_y[2]
        + DIFFUSE * laplace[1]
    )
    tracer_out = sea_mask * (fields[2] - ADVECT * advect[2] + DIFFUSE * laplace[2])
    return (zonal_out, merid_out, tracer_out)


def cut_axis(source, blocks):
    lead = source.shape[:-1]
    head_part = source[..., : TILE * blocks].reshape(lead + (blocks, TILE))
    tail_part = source[..., 4 : TILE * blocks + 4].reshape(lead + (blocks, TILE))[..., TILE - 4 :]
    return jnp.concatenate([head_part, tail_part], axis=-1)


def cut_rims(widened, blocks_y, blocks_x):
    by_column = cut_axis(widened, blocks_x)
    by_column = jnp.moveaxis(by_column, 1, -1)
    both_cut = cut_axis(by_column, blocks_y)
    both_cut = jnp.transpose(both_cut, (3, 1, 0, 4, 2))
    return both_cut.reshape(blocks_y * blocks_x, widened.shape[0], (TILE + 4) * (TILE + 4))


def remap_levels(pieces, edge_list):
    lower_edge = edge_list[:, :-1]
    upper_edge = edge_list[:, 1:]
    level_idx = jnp.arange(pieces.shape[1], dtype=jnp.int32)
    inside = (level_idx[None, None, :] >= lower_edge[..., None]) & (
        level_idx[None, None, :] < upper_edge[..., None]
    )
    weights = (
        inside.astype(jnp.float32)
        / jnp.maximum(upper_edge - lower_edge, 1).astype(jnp.float32)[..., None]
    )
    return jnp.einsum("nsk,nkc->nsc", weights, pieces, precision=lax.Precision.HIGHEST)


def interpolate(sigma_blocks):
    interp = jnp.asarray(cubic_weights(TILE), jnp.float32)
    return jnp.einsum("nsc,cj->nsj", sigma_blocks, interp, precision=lax.Precision.HIGHEST)


def per_device(zonal_velocity, meridional_velocity, tracer, land_mask, remap_bounds, nest_owner):
    levels, row_count, col_count = tracer.shape
    lon_count = lax.axis_size("lon")
    slot_count = CAP * lon_count
    fields = jnp.stack([zonal_velocity, meridional_velocity, tracer])
    lon_wide = padded(fields, (("lon", 3),), 1, True)
    lat_wide = padded(fields, (("lat", 2),), 1, False)
    global_rows = lax.axis_index("lat") * row_count + jnp.arange(row_count, dtype=jnp.int32)
    coriolis = coriolis_rows(global_rows)
    sea_mask = land_mask.astype(jnp.float32)
    zonal_out, merid_out, tracer_out = step_fields(
        fields,
        lon_wide[..., 2:],
        lon_wide[..., :-2],
        lat_wide[..., 2:, :],
        lat_wide[..., :-2, :],
        coriolis,
        sea_mask,
    )
    widened = padded(tracer_out, (("lon", 2),), 2, True)
    widened = padded(widened, (("lat", 1),), 2, False)
    rim_blocks = cut_rims(widened, BLK_Y, BLK_X)
    per_dev = BLK_Y * BLK_X
    owners = nest_owner.reshape(per_dev)
    bounds = remap_bounds.reshape(per_dev, SIGMA + 1)
    onehot = (owners[:, None] == jnp.arange(lon_count + 1, dtype=jnp.int32)[None, :]).astype(
        jnp.int32
    )
    before = jnp.cumsum(onehot, axis=0) - onehot
    rank_of = jnp.sum(before * onehot, axis=-1)
    target = jnp.where(owners < lon_count, owners * CAP + rank_of, slot_count)
    send_rims = (
        jnp.zeros((slot_count + 1, levels, RIM), jnp.float32)
        .at[target]
        .set(rim_blocks)[:slot_count]
    )
    send_bounds = (
        jnp.zeros((slot_count + 1, SIGMA + 1), jnp.int32).at[target].set(bounds)[:slot_count]
    )
    pieces = lax.all_to_all(
        send_rims.reshape(lon_count, CAP, levels, RIM),
        "lon",
        split_axis=0,
        concat_axis=0,
        tiled=True,
    )
    edge_list = lax.all_to_all(
        send_bounds.reshape(lon_count, CAP, SIGMA + 1),
        "lon",
        split_axis=0,
        concat_axis=0,
        tiled=True,
    )
    sources = pieces.shape[0]
    count = pieces.shape[1]
    sigma_blocks = remap_levels(
        pieces.reshape(sources * count, levels, RIM), edge_list.reshape(sources * count, SIGMA + 1)
    )
    received_tiles = interpolate(sigma_blocks).reshape(sources, count, SIGMA, NCELL)
    nest_tiles = received_tiles.reshape(1, 1, slot_count, SIGMA, NCELL)
    return (zonal_out, merid_out, tracer_out, nest_tiles)


def solution(mesh):
    return jax.shard_map(
        per_device,
        mesh=mesh,
        in_specs=(
            P(None, "lat", "lon"),
            P(None, "lat", "lon"),
            P(None, "lat", "lon"),
            P("lat", "lon"),
            P("lat", "lon", None),
            P("lat", "lon"),
        ),
        out_specs=(
            P(None, "lat", "lon"),
            P(None, "lat", "lon"),
            P(None, "lat", "lon"),
            P("lat", "lon", None, None, None),
        ),
        check_vma=False,
    )
```

profile of v0, /device:TPU:0, one launch (start us, length us, event | category | flops | bytes accessed | tf_op | source)
XLA Modules:
  0.0 292.7 jit_solution(11705517913162212534)
XLA Ops:
  0.6 5.4 %copy.96 = f32[75,24,384]{0,1,2:T(8,128)} copy(f32[75,24,384]{2,1,0:T(8,128)} %param.7) | data formatting | bytes 5529600 | tf_op args[0]
  9.5 5.2 %copy.89 = f32[75,24,384]{0,1,2:T(8,128)} copy(f32[75,24,384]{2,1,0:T(8,128)} %param.9) | data formatting | bytes 5529600 | tf_op args[2]
  14.7 11.2 %pad_maximum_fusion.12 = f32[3,75,24,384]{1,2,3,0:T(8,128)} fusion(f32[1,75,24,384]{1,2,3,0:T(8,128)} %bitcast.91, f32[1,75,24,384]{1,2,3,0:T(8,128)} %bitcast.88, f32[1,75,24,384]{1,2,3,0:T(8,128)} %bitcast.83), kind=kLoop, calls=%fused_computation.14 | loop fusion | flops 4147200 | bytes 16588800 | tf_op jit(solution)/shard_map/stack | solution.py:130
  25.8 5.4 %fusion.40 = (f32[3,75,1,384]{1,2,3,0:T(1,128)S(1)}, f32[3,75,1,384]{1,2,3,0:T(1,128)}) fusion(f32[3,75,24,384]{1,2,3,0:T(8,128)} %pad_maximum_fusion.12), kind=kLoop, calls=%fused_computation.81 | loop fusion | bytes 1382400 | tf_op jit(solution)/shard_map/slice | solution.py:31
  37.1 5.7 %collective-permute-start.3 = (f32[3,75,1,384]{3,2,1,0:T(1,128)}, f32[3,75,1,384]{3,2,1,0:T(1,128)S(1)}, u32[]{:S(2)}, u32[]{:S(2)}) collective-permute-start(f32[3,75,1,384]{3,2,1,0:T(1,128)} %copy.93), channel_id=1, source_target_pairs={{0,1},{1,2},{2,3},{4,5},{5,6},{6,7},{8,9},{9,10},{10,11},{12,13},{... | collective-permute-start | bytes 1036808 | tf_op jit(solution)/shard_map/ppermute | solution.py:33
  48.8 5.3 %copy.90 = f32[75,24,384]{0,1,2:T(8,128)} copy(f32[75,24,384]{2,1,0:T(8,128)} %broadcast_multiply_fusion.1) | data formatting | bytes 5529600 | tf_op jit(solution)/shard_map/mul | solution.py:73
  60.3 37.2 %multiply_subtract_fusion = f32[3,75,24,384]{1,2,3,0:T(8,128)} fusion(f32[3,75,24,1]{1,2,3,0:T(8,128)S(1)} %collective-permute-done, f32[1,75,24,384]{1,2,3,0:T(8,128)} %bitcast.92, f32[1,75,24,384]{1,2,3,0:T(8,128)} %bitcast.89, f32[1,75,24,384]{1,2,3,0:T(8,128)} %bitcast.84, f32[3,75,24,1]{1,2,3,0:T(8,128)S(1)} %collective-permute-done.1, ...), kind=kLoop, calls=%fused_computation.15 | loop fusion | flops 39398400 | bytes 17323200 | tf_op jit(solution)/shard_map/sub | solution.py:72
  97.5 36.2 %multiply_add_fusion = (f32[3,75,24,384]{1,2,3,0:T(8,128)}, f32[3,75,24,384]{1,2,3,0:T(8,128)}, f32[3,75,24,384]{1,2,3,0:T(8,128)}) fusion(f32[75,24,384]{0,1,2:T(8,128)} %copy.95, f32[75,24,384]{0,1,2:T(8,128)} %copy.90, f32[1,75,24,384]{1,2,3,0:T(8,128)} %bitcast.93, f32[1,75,24,384]{1,2,3,0:T(8,128)} %bitcast.90, f32[1,75,24,384]{1,2,3,0:T(8,128)S(1)} %bitcast.87, ...), kind=kLoop, calls=%fused_computation.16 | loop fusion | flops 35251200 | bytes 39441600 | tf_op jit(solution)/shard_map/add | solution.py:73
  133.7 22.3 %fusion.9 = (f32[75,24,384]{0,1,2:T(8,128)}, f32[75,24,384]{0,1,2:T(8,128)}, f32[75,24,384]{0,1,2:T(8,128)}) fusion(f32[3,75,24,384]{1,2,3,0:T(8,128)} %multiply_subtract_fusion, f32[3,75,24,384]{1,2,3,0:T(8,128)} %get-tuple-element.29, f32[75,24,384]{0,1,2:T(8,128)} %copy.88, f32[3,75,24,384]{1,2,3,0:T(8,128)} %get-tuple-element.28, ...), kind=kLoop, calls=%fused_computation.32 | loop fusion | flops 17280000 | bytes 38744160 | tf_op jit(solution)/shard_map/mul | solution.py:81
  164.3 4.3 %collective-permute-start.6 = (f32[75,2,388]{2,0,1:T(8,128)S(1)}, f32[75,2,388]{2,0,1:T(8,128)S(1)}, u32[]{:S(2)}, u32[]{:S(2)}) collective-permute-start(f32[75,2,388]{2,0,1:T(8,128)S(1)} %copy.102), channel_id=1, source_target_pairs={{0,1},{1,2},{2,3},{4,5},{5,6},{6,7},{8,9},{9,10},{10,11},{12,13},{... | collective-permute-start | bytes 698408 | tf_op jit(solution)/shard_map/ppermute | solution.py:33
  171.9 4.5 %all-to-all-start = ((s32[8,2,31]{2,1,0:T(2,128)}), s32[8,2,31]{2,1,0:T(2,128)S(1)}, u32[]{:S(2)}, u32[]{:S(2)}) async-start(s32[8,2,31]{2,1,0:T(2,128)} %bitcast.14), calls=%async_computation | async-start | bytes 16384 | tf_op jit(solution)/shard_map/all_to_all | solution.py:172
  177.4 4.9 %collective-permute-done.7 = f32[75,2,388]{2,0,1:T(8,128)S(1)} collective-permute-done((f32[75,2,388]{2,0,1:T(8,128)S(1)}, f32[75,2,388]{2,0,1:T(8,128)S(1)}, u32[]{:S(2)}, u32[]{:S(2)}) %collective-permute-start.7) | collective-permute-done | bytes 232832 | tf_op jit(solution)/shard_map/ppermute | solution.py:34
  183.3 4.6 %pad_maximum_fusion.13 = f32[75,28,388]{0,1,2:T(8,128)S(1)} fusion(f32[75,2,388]{0,1,2:T(2,128)} %copy.105, f32[75,24,2]{0,1,2:T(8,128)S(1)} %collective-permute-done.5, f32[75,24,384]{0,1,2:T(8,128)} %get-tuple-element.33, f32[75,24,2]{0,1,2:T(8,128)S(1)} %collective-permute-done.4, f32[75,2,388]{0,1,2:T(2,128)} %copy.104), kind=kLoop, calls=%fused_computation.21 | loop fusion | flops 3259200 | bytes 6518400 | tf_op jit(solution)/shard_map/concatenate | solution.py:35
  187.9 6.1 %fusion.43 = (f32[75,28,384]{0,1,2:T(8,128)}, f32[75,28,384]{0,1,2:T(8,128)}) fusion(f32[75,28,388]{0,1,2:T(8,128)S(1)} %pad_maximum_fusion.13), kind=kLoop, calls=%fused_computation.84 | loop fusion | bytes 12902400 | tf_op jit(solution)/shard_map/slice | solution.py:94
  195.9 7.6 %maximum_bitcast_fusion = f32[75,32,16,28]{0,3,2,1:T(8,128)} fusion(f32[75,28,32,4]{0,1,3,2:T(8,128)S(1)} %slice.143, f32[75,28,32,12]{0,1,3,2:T(8,128)} %bitcast.98), kind=kLoop, calls=%fused_computation.17 | loop fusion | flops 1075200 | bytes 8601600 | tf_op jit(solution)/shard_map/transpose | solution.py:101
  203.5 11.8 %fusion.42 = (f32[75,32,16,24]{0,3,2,1:T(8,128)}, f32[75,32,16,24]{0,3,2,1:T(8,128)}) fusion(f32[75,32,16,28]{0,3,2,1:T(8,128)} %maximum_bitcast_fusion), kind=kLoop, calls=%fused_computation.83 | loop fusion | bytes 14745600 | tf_op jit(solution)/shard_map/slice | solution.py:94
  215.3 4.1 %copy.107 = f32[75,32,16,24]{0,2,3,1:T(8,128)S(1)} copy(f32[75,32,16,24]{0,3,2,1:T(8,128)} %get-tuple-element.39) | data formatting | bytes 7372800 | tf_op jit(solution)/shard_map/slice | solution.py:95
  232.5 8.5 %copy.109 = f32[64,75,256]{2,1,0:T(8,128)} copy(f32[64,75,256]{1,2,0:T(8,128)} %bitcast.94) | data formatting | bytes 9830400 | tf_op jit(solution)/shard_map/reshape | solution.py:104
  241.2 7.8 %scatter_fusion = f32[17,75,256]{2,1,0:T(8,128)S(1)} fusion(f32[17,75,256]{2,1,0:T(8,128)S(1)} %broadcast_in_dim.10, s32[64]{0:T(128)S(1)} %fusion.36, f32[64,75,256]{2,1,0:T(8,128)} %copy.109), kind=kCustom, calls=%fused_computation.1 | custom fusion | bytes 14745856 | tf_op jit(solution)/shard_map/scatter | solution.py:160
  251.1 4.2 %all-to-all-start.1 = ((f32[8,2,75,256]{3,1,2,0:T(2,128)}), f32[8,2,75,256]{3,1,2,0:T(2,128)S(1)}, u32[]{:S(2)}, u32[]{:S(2)}) async-start(f32[8,2,75,256]{3,1,2,0:T(2,128)} %copy.110), calls=%async_computation.1 | async-start | bytes 2457600 | tf_op jit(solution)/shard_map/all_to_all | solution.py:165
  255.4 5.5 %copy.114 = f32[75,24,384]{2,1,0:T(8,128)} copy(f32[75,24,384]{0,1,2:T(8,128)} %get-tuple-element.33) | data formatting | bytes 5529600
  260.8 5.4 %copy.112 = f32[75,24,384]{2,1,0:T(8,128)} copy(f32[75,24,384]{0,1,2:T(8,128)} %get-tuple-element.32) | data formatting | bytes 5529600
  266.3 5.6 %copy.113 = f32[75,24,384]{2,1,0:T(8,128)} copy(f32[75,24,384]{0,1,2:T(8,128)} %get-tuple-element.31) | data formatting | bytes 5529600
  271.8 13.9 %all-to-all-done.1 = f32[8,2,75,256]{3,1,2,0:T(2,128)S(1)} async-done(((f32[8,2,75,256]{3,1,2,0:T(2,128)}), f32[8,2,75,256]{3,1,2,0:T(2,128)S(1)}, u32[]{:S(2)}, u32[]{:S(2)}) %all-to-all-start.1) | async-done | bytes 1228832 | tf_op jit(solution)/shard_map/all_to_all | solution.py:165
  (81 shorter events, 59.1 us)
Async XLA Ops:
  0.6 5.4 %copy-start.1 = (f32[75,24,384]{2,1,0:T(8,128)S(1)}, f32[75,24,384]{2,1,0:T(8,128)}, u32[]{:S(2)}) copy-start(f32[75,24,384]{2,1,0:T(8,128)} %param.8) | copy-start | bytes 8294404
  14.7 32.0 %copy-start = (f32[75,24,384]{2,1,0:T(8,128)S(1)}, f32[75,24,384]{2,1,0:T(8,128)}, u32[]{:S(2)}) copy-start(f32[75,24,384]{2,1,0:T(8,128)} %param.7) | copy-start | bytes 8294404
  34.0 14.5 %copy-start.6 = (s32[2,32]{1,0:T(2,128)S(1)}, s32[2,32]{1,0:T(2,128)}, u32[]{:S(2)}) copy-start(s32[2,32]{1,0:T(2,128)} %param.12) | copy-start | bytes 772
  34.0 23.5 %collective-permute-start.2 = (f32[3,75,1,384]{3,2,1,0:T(1,128)}, f32[3,75,1,384]{3,2,1,0:T(1,128)}, u32[]{:S(2)}, u32[]{:S(2)}) collective-permute-start(f32[3,75,1,384]{3,2,1,0:T(1,128)} %copy.91), channel_id=1, source_target_pairs={{1,0},{2,1},{3,2},{5,4},{6,5},{7,6},{9,8},{10,9},{11,10},{13,12},{... | collective-permute-start | bytes 1036808 | tf_op jit(solution)/shard_map/ppermute | solution.py:34
  37.1 11.3 %copy-start.2 = (f32[75,24,384]{2,1,0:T(8,128)S(1)}, f32[75,24,384]{2,1,0:T(8,128)}, u32[]{:S(2)}) copy-start(f32[75,24,384]{2,1,0:T(8,128)} %param.8) | copy-start | bytes 8294404
  37.1 22.6 %collective-permute-start.3 = (f32[3,75,1,384]{3,2,1,0:T(1,128)}, f32[3,75,1,384]{3,2,1,0:T(1,128)S(1)}, u32[]{:S(2)}, u32[]{:S(2)}) collective-permute-start(f32[3,75,1,384]{3,2,1,0:T(1,128)} %copy.93), channel_id=1, source_target_pairs={{0,1},{1,2},{2,3},{4,5},{5,6},{6,7},{8,9},{9,10},{10,11},{12,13},{... | collective-permute-start | bytes 1036808 | tf_op jit(solution)/shard_map/ppermute | solution.py:33
  43.6 16.6 %collective-permute-start = (f32[3,75,24,1]{1,2,3,0:T(8,128)S(1)}, f32[3,75,24,1]{1,2,3,0:T(8,128)S(1)}, u32[]{:S(2)}, u32[]{:S(2)}) collective-permute-start(f32[3,75,24,1]{1,2,3,0:T(8,128)S(1)} %get-tuple-element.37), channel_id=1, source_target_pairs={{4,0},{8,4},{12,8},{16,12},{20,16},{24,20},{28,24},{0,28},{5,1},{9... | collective-permute-start | bytes 64808 | tf_op jit(solution)/shard_map/ppermute | solution.py:34
  46.6 13.7 %collective-permute-start.1 = (f32[3,75,24,1]{1,2,3,0:T(8,128)S(1)}, f32[3,75,24,1]{1,2,3,0:T(8,128)S(1)}, u32[]{:S(2)}, u32[]{:S(2)}) collective-permute-start(f32[3,75,24,1]{1,2,3,0:T(8,128)S(1)} %get-tuple-element.36), channel_id=1, source_target_pairs={{0,4},{4,8},{8,12},{12,16},{16,20},{20,24},{24,28},{28,0},{1,5},{5... | collective-permute-start | bytes 64808 | tf_op jit(solution)/shard_map/ppermute | solution.py:33
  48.8 8.7 %copy-start.4 = (s32[24,384]{1,0:T(8,128)S(1)}, s32[24,384]{1,0:T(8,128)}, u32[]{:S(2)}) copy-start(s32[24,384]{1,0:T(8,128)} %param.10) | copy-start | bytes 110596
  59.7 37.8 %slice-start = ((s8[4718592]{0:T(1024)(128)(4,1)}), s8[524288]{0:T(1024)(128)(4,1)S(1)}, s32[]{:S(2)}) async-start(s8[4718592]{0:T(1024)(128)(4,1)} %bitcast.85), calls=%async_computation.2 | async-start | bytes 1048576
  60.3 37.3 %slice-start.1 = ((s8[4718592]{0:T(1024)(128)(4,1)}), s8[4194304]{0:T(1024)(128)(4,1)S(1)}, s32[]{:S(2)}) async-start(s8[4718592]{0:T(1024)(128)(4,1)} %bitcast.85), calls=%async_computation.3 | async-start | bytes 8388608
  155.9 14.5 %copy-start.5 = (s32[2,32,31]{1,0,2:T(2,128)S(1)}, s32[2,32,31]{1,0,2:T(2,128)}, u32[]{:S(2)}) copy-start(s32[2,32,31]{1,0,2:T(2,128)} %param.11) | copy-start | bytes 23812
  156.7 5.0 %collective-permute-start.4 = (f32[75,24,2]{0,1,2:T(8,128)S(1)}, f32[75,24,2]{0,1,2:T(8,128)S(1)}, u32[]{:S(2)}, u32[]{:S(2)}) collective-permute-start(f32[75,24,2]{0,1,2:T(8,128)S(1)} %get-tuple-element.44), channel_id=1, source_target_pairs={{0,4},{4,8},{8,12},{12,16},{16,20},{20,24},{24,28},{28,0},{1,5},{5... | collective-permute-start | bytes 43208 | tf_op jit(solution)/shard_map/ppermute | solution.py:33
  156.7 5.1 %collective-permute-start.5 = (f32[75,24,2]{0,1,2:T(8,128)S(1)}, f32[75,24,2]{0,1,2:T(8,128)S(1)}, u32[]{:S(2)}, u32[]{:S(2)}) collective-permute-start(f32[75,24,2]{0,1,2:T(8,128)S(1)} %get-tuple-element.45), channel_id=1, source_target_pairs={{4,0},{8,4},{12,8},{16,12},{20,16},{24,20},{28,24},{0,28},{5,1},{9... | collective-permute-start | bytes 43208 | tf_op jit(solution)/shard_map/ppermute | solution.py:34
  164.3 12.1 %collective-permute-start.6 = (f32[75,2,388]{2,0,1:T(8,128)S(1)}, f32[75,2,388]{2,0,1:T(8,128)S(1)}, u32[]{:S(2)}, u32[]{:S(2)}) collective-permute-start(f32[75,2,388]{2,0,1:T(8,128)S(1)} %copy.102), channel_id=1, source_target_pairs={{0,1},{1,2},{2,3},{4,5},{5,6},{6,7},{8,9},{9,10},{10,11},{12,13},{... | collective-permute-start | bytes 698408 | tf_op jit(solution)/shard_map/ppermute | solution.py:33
  168.8 13.5 %collective-permute-start.7 = (f32[75,2,388]{2,0,1:T(8,128)S(1)}, f32[75,2,388]{2,0,1:T(8,128)S(1)}, u32[]{:S(2)}, u32[]{:S(2)}) collective-permute-start(f32[75,2,388]{2,0,1:T(8,128)S(1)} %copy.103), channel_id=1, source_target_pairs={{1,0},{2,1},{3,2},{5,4},{6,5},{7,6},{9,8},{10,9},{11,10},{13,12},{... | collective-permute-start | bytes 698408 | tf_op jit(solution)/shard_map/ppermute | solution.py:34
  171.9 79.2 %all-to-all-start = ((s32[8,2,31]{2,1,0:T(2,128)}), s32[8,2,31]{2,1,0:T(2,128)S(1)}, u32[]{:S(2)}, u32[]{:S(2)}) async-start(s32[8,2,31]{2,1,0:T(2,128)} %bitcast.14), calls=%async_computation | async-start | bytes 16384 | tf_op jit(solution)/shard_map/all_to_all | solution.py:172
  215.3 5.6 %slice-start.2 = ((s8[6291456]{0:T(1024)(128)(4,1)}), s8[4194304]{0:T(1024)(128)(4,1)S(1)}, s32[]{:S(2)}) async-start(s8[6291456]{0:T(1024)(128)(4,1)} %bitcast.95), calls=%async_computation.4 | async-start | bytes 8388608
  215.3 5.6 %slice-start.3 = ((s8[6291456]{0:T(1024)(128)(4,1)}), s8[2097152]{0:T(1024)(128)(4,1)S(1)}, s32[]{:S(2)}) async-start(s8[6291456]{0:T(1024)(128)(4,1)} %bitcast.95), calls=%async_computation.5 | async-start | bytes 4194304
  251.1 34.6 %all-to-all-start.1 = ((f32[8,2,75,256]{3,1,2,0:T(2,128)}), f32[8,2,75,256]{3,1,2,0:T(2,128)S(1)}, u32[]{:S(2)}, u32[]{:S(2)}) async-start(f32[8,2,75,256]{3,1,2,0:T(2,128)} %copy.110), calls=%async_computation.1 | async-start | bytes 2457600 | tf_op jit(solution)/shard_map/all_to_all | solution.py:165
  266.3 20.5 %copy-start.3 = (f32[256,1296,1]{0,1,2:T(8,128)S(1)}, f32[256,1296,1]{0,1,2:T(8,128)}, u32[]{:S(2)}) copy-start(f32[256,1296,1]{0,1,2:T(8,128)} %constant.50) | copy-start | bytes 3981316
where the time goes:
time: 294 us; the launch traced here: 293 us
  other arithmetic  128 us (44%)
  local copies, waits for them, and re-layouts  112 us (38%)
  starting transfers between devices  28 us (10%)
  waiting for transfers between devices  20.3 us (7%)
  matrix products  3.7 us (1%)
    sub x1, other arithmetic, step_fields(): laplace = east_cell + west_cell + north_cell + south_cell - 4.0 * fields  37.2 us
    add x1, other arithmetic, step_fields(): advect = zonal_vel[None] * grad_x + merid_vel[None] * grad_y  36.2 us
    unnamed x29, local copies, waits for them, and re-layouts  33.6 us
    mul x1, other arithmetic, step_fields(): sea_mask * (merid_vel - ADVECT * advect[1] - coriolis * zonal_vel - PRESS...  22.3 us
    slice x3, local copies, waits for them, and re-layouts, cut_axis(): head_part = source[..., :TILE * blocks].reshape(lead + (blocks, TILE))  21.7 us
    all_to_all x1, waiting for transfers between devices, per_device(): lax.all_to_all(send_rims.reshape(lon_count, CAP, levels, RIM), 'lon', spl...  13.9 us
    another operation x1, other arithmetic, per_device(): fields = jnp.stack([zonal_velocity, meridional_velocity, tracer])  11.2 us
    ppermute x4, starting transfers between devices, padded(): before = lax.ppermute(last, axis, up)  10 us
  transfers between devices with their start and end apart: 10, of which 4 were waited for; matrix products, arithmetic and copies ran while one was open for 36% of the time, Pallas kernels for 0%

commit v1 on v0

v1 whole, which is shorter than its diff:
```python
import functools
import math

import jax
import jax.numpy as jnp
import numpy as np
from jax import lax
from jax.experimental import pallas as pl
from jax.experimental.pallas import tpu as pltpu
from jax.sharding import PartitionSpec as P

SIGMA = 30
SIGMA_PAD = 32
TILE = 12
CAP = 2
BLK_X = 32
BLK_Y = 2
RIM = 256
NCELL = 1296
LEVEL_PAD = 80
CHUNK = 15

ADVECT = 0.25
DIFFUSE = 0.15
PRESSURE = 0.3
ROTATION = 0.6
BASE_LATITUDE = 20.0
ROW_DEGREES = 1.0 / 12.0

PARAMS = pltpu.CompilerParams(vmem_limit_bytes=48 * 2**20)


def cubic_weights(tile_cells):
    span_len = tile_cells + 4
    weights = np.zeros((span_len, 3 * tile_cells), np.float32)
    for cell_idx in range(tile_cells):
        for phase_idx in range(3):
            if phase_idx == 0:
                base_cell, fraction = (cell_idx - 1, 2.0 / 3.0)
            elif phase_idx == 1:
                base_cell, fraction = (cell_idx, 0.0)
            else:
                base_cell, fraction = (cell_idx, 1.0 / 3.0)
            coeffs = (
                (-(fraction**3) + 2 * fraction**2 - fraction) / 2,
                (3 * fraction**3 - 5 * fraction**2 + 2) / 2,
                (-3 * fraction**3 + 4 * fraction**2 + fraction) / 2,
                (fraction**3 - fraction**2) / 2,
            )
            for offset in range(4):
                weights[base_cell + 1 + offset, 3 * cell_idx + phase_idx] += coeffs[offset]
    return np.kron(weights, weights).astype(np.float32)


def coriolis_rows(row_index):
    degrees = BASE_LATITUDE + (row_index.astype(jnp.float32) + 0.5) * ROW_DEGREES
    latitude = degrees * (math.pi / 180.0)
    return (ROTATION * jnp.sin(latitude))[:, None]


def whole(shape):
    return pl.BlockSpec(shape, lambda i: (0,) * len(shape))


def pack_kernel(u_ref, v_ref, t_ref, first_row, last_row, first_col, last_col):
    step = pl.program_id(0)
    rows, cols = u_ref.shape[1:]
    lane = lax.broadcasted_iota(jnp.int32, (rows, 128), 1)

    @pl.when(step == 0)
    def _():
        first_row[...] = jnp.zeros_like(first_row)
        last_row[...] = jnp.zeros_like(last_row)
        first_col[...] = jnp.zeros_like(first_col)
        last_col[...] = jnp.zeros_like(last_col)

    for f, ref in enumerate((u_ref, v_ref, t_ref)):
        west = first_col[f]
        east = last_col[f]
        for i in range(CHUNK):
            k = step * CHUNK + i
            first_row[pl.ds(f * LEVEL_PAD + k, 1), :] = ref[i, 0:1, :]
            last_row[pl.ds(f * LEVEL_PAD + k, 1), :] = ref[i, rows - 1 : rows, :]
            here = lane == k
            west = jnp.where(here, ref[i, :, 0:128][:, 0:1], west)
            east = jnp.where(here, ref[i, :, cols - 128 : cols][:, 127:128], east)
        first_col[f] = west
        last_col[f] = east


def neighbours(x, f, k, east_ref, west_ref, north_ref, south_ref):
    rows, cols = x.shape
    col = lax.broadcasted_iota(jnp.int32, (rows, cols), 1)
    row = lax.broadcasted_iota(jnp.int32, (rows, cols), 0)
    e_col = pltpu.roll(east_ref[f], 127 - k, axis=1)[:, 127:128]
    w_col = pltpu.roll(west_ref[f], 127 - k, axis=1)[:, 127:128]
    n_row = north_ref[pl.ds(f * LEVEL_PAD + k, 1), :]
    s_row = south_ref[pl.ds(f * LEVEL_PAD + k, 1), :]
    east = jnp.where(col == cols - 1, e_col, pltpu.roll(x, cols - 1, axis=1))
    west = jnp.where(col == 0, w_col, pltpu.roll(x, 1, axis=1))
    north = jnp.where(row == rows - 1, n_row, pltpu.roll(x, rows - 1, axis=0))
    south = jnp.where(row == 0, s_row, pltpu.roll(x, 1, axis=0))
    return 0.5 * (east - west), 0.5 * (north - south), east + west + north + south - 4.0 * x


def tracer_kernel(
    u_ref, v_ref, t_ref, mask_ref, east_ref, west_ref, north_ref, south_ref,
    out_ref, tiles, low_rows, high_rows, west_cols, east_cols,
):
    step = pl.program_id(0)
    rows, cols = u_ref.shape[1:]
    sea = mask_ref[...].astype(jnp.float32)
    for i in range(CHUNK):
        k = step * CHUNK + i
        t = t_ref[i]
        gx, gy, lap = neighbours(t, 2, k, east_ref, west_ref, north_ref, south_ref)
        advect = u_ref[i] * gx + v_ref[i] * gy
        new = sea * (t - ADVECT * advect + DIFFUSE * lap)
        out_ref[i] = new
        for c in range(cols // 128):
            tiles[c, pl.ds(pl.multiple_of(k * rows, 8), rows), :] = new[:, c * 128 : c * 128 + 128]

    @pl.when(step == pl.num_programs(0) - 1)
    def _():
        count = tiles.shape[1] // rows
        lane = lax.broadcasted_iota(jnp.int32, (count, 128), 1)
        low_rows[...] = jnp.zeros_like(low_rows)
        high_rows[...] = jnp.zeros_like(high_rows)
        west_cols[...] = jnp.zeros_like(west_cols)
        east_cols[...] = jnp.zeros_like(east_cols)
        for r in range(2):
            for c in range(0, cols, 128):
                low_rows[r * LEVEL_PAD : r * LEVEL_PAD + count, c : c + 128] = tiles[
                    c // 128, pl.ds(r, count, stride=rows), :
                ]
                high_rows[r * LEVEL_PAD : r * LEVEL_PAD + count, c : c + 128] = tiles[
                    c // 128, pl.ds(rows - 2 + r, count, stride=rows), :
                ]
        west = jnp.zeros((count, 128), jnp.float32)
        east = jnp.zeros((count, 128), jnp.float32)
        for r in range(rows):
            here = (lane >= 2 * r) & (lane < 2 * r + 2)
            w = tiles[0, pl.ds(r, count, stride=rows), :]
            e = tiles[cols // 128 - 1, pl.ds(r, count, stride=rows), :]
            west = jnp.where(here, pltpu.roll(w, 2 * r, axis=1) if r else w, west)
            east = jnp.where(here, pltpu.roll(e, 2 * r + 2, axis=1), east)
        west_cols[0:count, :] = west
        east_cols[0:count, :] = east


def momentum_kernel(
    u_ref, v_ref, t_ref, mask_ref, coriolis_ref, east_ref, west_ref, north_ref, south_ref,
    zonal_ref, merid_ref,
):
    step = pl.program_id(0)
    sea = mask_ref[...].astype(jnp.float32)
    coriolis = coriolis_ref[...]
    halos = (east_ref, west_ref, north_ref, south_ref)
    for i in range(CHUNK):
        k = step * CHUNK + i
        u, v = u_ref[i], v_ref[i]
        t_gx, t_gy, _ = neighbours(t_ref[i], 2, k, *halos)
        gx, gy, lap = neighbours(u, 0, k, *halos)
        zonal_ref[i] = sea * (
            u - ADVECT * (u * gx + v * gy) + coriolis * v - PRESSURE * t_gx + DIFFUSE * lap
        )
        gx, gy, lap = neighbours(v, 1, k, *halos)
        merid_ref[i] = sea * (
            v - ADVECT * (u * gx + v * gy) - coriolis * u - PRESSURE * t_gy + DIFFUSE * lap
        )


def rim_kernel(
    block_ref, x_ref, east_ref, west_ref, north_ref, south_ref, corner_n, corner_s, inside_ref,
    out_ref, wide, rim,
):
    levels = inside_ref.shape[2]
    cols = x_ref.shape[0] * 128
    rows = x_ref.shape[1] // levels
    lane = lax.broadcasted_iota(jnp.int32, (levels, 128), 1)

    def side(east, west, r):
        e = pltpu.roll(east, 128 - 2 * r, axis=1) if r else east
        w = pltpu.roll(west, 126 - 2 * r, axis=1)
        return jnp.where(lane < 64, e, w)

    for r in range(rows):
        for c in range(0, cols, 128):
            wide[r + 2, 0:levels, c : c + 128] = x_ref[c // 128, pl.ds(r, levels, stride=rows), :]
        wide[r + 2, 0:levels, cols : cols + 128] = side(
            east_ref[0:levels, :], west_ref[0:levels, :], r
        )
    for j in range(2):
        at = slice(j * LEVEL_PAD, j * LEVEL_PAD + levels)
        wide[j, 0:levels, 0:cols] = south_ref[at, :]
        wide[j, 0:levels, cols : cols + 128] = side(
            corner_s[0, 0:levels, :], corner_s[1, 0:levels, :], rows - 2 + j
        )
        wide[rows + 2 + j, 0:levels, 0:cols] = north_ref[at, :]
        wide[rows + 2 + j, 0:levels, cols : cols + 128] = side(
            corner_n[0, 0:levels, :], corner_n[1, 0:levels, :], j
        )

    ring = cols + 128

    def slot(s, carry):
        b = block_ref[s]
        by, bx = b // BLK_X, b % BLK_X
        start = (TILE * bx - 2 + ring) % ring
        first, off = start // 128, start % 128
        second = (first + 1) % (ring // 128)
        first = pl.multiple_of(first * 128, 128)
        second = pl.multiple_of(second * 128, 128)
        for half in range(2):
            acc = jnp.zeros((levels, 128), jnp.float32)
            for q in range(8):
                r = by * TILE + half * 8 + q
                a = wide[r, 0:levels, pl.ds(first, 128)]
                z = wide[r, 0:levels, pl.ds(second, 128)]
                both = jnp.where(lane >= off, a, z)
                both = pltpu.roll(both, (16 * q - off + 128) % 128, axis=1)
                acc = jnp.where((lane >= 16 * q) & (lane < 16 * q + 16), both, acc)
            rim[0:levels, half * 128 : half * 128 + 128] = acc
        inside = inside_ref[s]
        x = rim[0:levels, :]
        high = x.astype(jnp.bfloat16)
        low = (x - high.astype(jnp.float32)).astype(jnp.bfloat16)
        ones = inside.astype(jnp.bfloat16)
        total = jnp.dot(ones, high, preferred_element_type=jnp.float32) + jnp.dot(
            ones, low, preferred_element_type=jnp.float32
        )
        count = jnp.sum(inside, axis=1, keepdims=True)
        total = total / jnp.maximum(count, 1.0)
        out_ref[s, 0] = total[:, 0:128]
        out_ref[s, 1] = total[:, 128:256]
        return carry

    lax.fori_loop(0, out_ref.shape[0], slot, 0)


def interp_kernel(x_ref, high_ref, low_ref, out_ref):
    slots = x_ref.shape[0] // (2 * SIGMA_PAD)
    per_step = out_ref.shape[0] // slots
    step = pl.program_id(0)
    for i in range(per_step):
        s = step * per_step + i
        halves = [
            x_ref[pl.ds(h * SIGMA_PAD + s, slots, stride=2 * SIGMA_PAD), :] for h in range(2)
        ]
        x = jnp.concatenate(halves, axis=1)
        high = x.astype(jnp.bfloat16)
        low = (x - high.astype(jnp.float32)).astype(jnp.bfloat16)
        both = jnp.concatenate([high, low], axis=0)
        wide = jnp.dot(both, high_ref[...], preferred_element_type=jnp.float32)
        out_ref[i * slots : (i + 1) * slots, :] = (
            wide[:slots]
            + wide[slots:]
            + jnp.dot(high, low_ref[...], preferred_element_type=jnp.float32)
        )


def shift(x, axis, wrap, forward):
    count = lax.axis_size(axis)
    up = [(i, (i + 1) % count) for i in range(count if wrap else count - 1)]
    return lax.ppermute(x, axis, up if forward else [(j, i) for i, j in up])


def per_device(zonal_velocity, meridional_velocity, tracer, land_mask, remap_bounds, nest_owner):
    levels, rows, cols = tracer.shape
    lon_count = lax.axis_size("lon")
    slots = CAP * lon_count
    steps = levels // CHUNK
    f32 = jnp.float32
    fields = (zonal_velocity, meridional_velocity, tracer)
    field_spec = pl.BlockSpec((CHUNK, rows, cols), lambda i: (i, 0, 0))
    row_shape, col_shape = (3 * LEVEL_PAD, cols), (3, rows, 128)
    field_bytes = levels * rows * cols * 4

    first_row, last_row, first_col, last_col = pl.pallas_call(
        pack_kernel,
        grid=(steps,),
        in_specs=[field_spec] * 3,
        out_specs=[whole(row_shape)] * 2 + [whole(col_shape)] * 2,
        out_shape=[jax.ShapeDtypeStruct(row_shape, f32)] * 2
        + [jax.ShapeDtypeStruct(col_shape, f32)] * 2,
        compiler_params=PARAMS,
        name="pack_edges",
    )(*fields)
    north = shift(first_row, "lat", False, False)
    south = shift(last_row, "lat", False, True)
    east = shift(first_col, "lon", True, False)
    west = shift(last_col, "lon", True, True)
    halos = (east, west, north, south)
    halo_specs = [whole(col_shape)] * 2 + [whole(row_shape)] * 2

    margin_row, margin_col = (2 * LEVEL_PAD, cols), (LEVEL_PAD, 128)
    tile_shape = (cols // 128, levels * rows, 128)
    tracer_new, tiles, low_rows, high_rows, west_cols, east_cols = pl.pallas_call(
        tracer_kernel,
        grid=(steps,),
        in_specs=[field_spec] * 3 + [whole((rows, cols))] + halo_specs,
        out_specs=[field_spec, whole(tile_shape)] + [whole(margin_row)] * 2 + [whole(margin_col)] * 2,
        out_shape=[jax.ShapeDtypeStruct(s, f32) for s in (tracer.shape, tile_shape)]
        + [jax.ShapeDtypeStruct(margin_row, f32)] * 2
        + [jax.ShapeDtypeStruct(margin_col, f32)] * 2,
        compiler_params=PARAMS,
        name="tracer_step",
    )(*fields, land_mask, *halos)
    east_margin = shift(west_cols, "lon", True, False)
    west_margin = shift(east_cols, "lon", True, True)
    north_margin = shift(low_rows, "lat", False, False)
    south_margin = shift(high_rows, "lat", False, True)
    sides = jnp.stack([east_margin, west_margin])
    corner_n = shift(sides, "lat", False, False)
    corner_s = shift(sides, "lat", False, True)

    row_index = lax.axis_index("lat") * rows + jnp.arange(rows, dtype=jnp.int32)
    coriolis = jnp.broadcast_to(coriolis_rows(row_index), (rows, cols))
    zonal_new, merid_new = pl.pallas_call(
        momentum_kernel,
        grid=(steps,),
        in_specs=[field_spec] * 3 + [whole((rows, cols))] * 2 + halo_specs,
        out_specs=[field_spec] * 2,
        out_shape=[jax.ShapeDtypeStruct(tracer.shape, f32)] * 2,
        compiler_params=PARAMS,
        cost_estimate=pl.CostEstimate(
            flops=60 * levels * rows * cols, bytes_accessed=5 * field_bytes, transcendentals=0
        ),
        name="momentum_step",
    )(*fields, land_mask, coriolis, *halos)

    per_dev = BLK_Y * BLK_X
    owners = nest_owner.reshape(per_dev)
    bounds = remap_bounds.reshape(per_dev, SIGMA + 1)
    number = jnp.arange(per_dev, dtype=jnp.int32)
    earlier = (owners[None, :] == owners[:, None]) & (number[None, :] < number[:, None])
    rank_of = jnp.sum(earlier.astype(jnp.int32), axis=1)
    target = jnp.where(owners < lon_count, owners * CAP + rank_of, slots)
    chosen = (target[None, :] == jnp.arange(slots, dtype=jnp.int32)[:, None]).astype(jnp.int32)
    block_of = jnp.sum(chosen * number[None, :], axis=1)
    edges = jnp.sum(chosen[:, :, None] * bounds[None], axis=1)
    edges = jnp.pad(edges, ((0, 0), (0, SIGMA_PAD - SIGMA)), mode="edge")
    level = jnp.arange(levels, dtype=jnp.int32)[None, None, :]
    inside = ((level >= edges[:, :-1, None]) & (level < edges[:, 1:, None])).astype(f32)

    vmem = pl.BlockSpec(memory_space=pltpu.VMEM)
    sigma_blocks = pl.pallas_call(
        rim_kernel,
        in_specs=[pl.BlockSpec(memory_space=pltpu.SMEM)] + [vmem] * 8,
        out_specs=vmem,
        out_shape=jax.ShapeDtypeStruct((slots, 2, SIGMA_PAD, 128), f32),
        scratch_shapes=[
            pltpu.VMEM((rows + 4, LEVEL_PAD, cols + 128), f32),
            pltpu.VMEM((LEVEL_PAD, RIM), f32),
        ],
        compiler_params=PARAMS,
        name="sigma_rims",
    )(
        block_of, tiles, east_margin, west_margin, north_margin, south_margin,
        corner_n, corner_s,
        jnp.pad(inside, ((0, 0), (0, SIGMA_PAD - inside.shape[1]), (0, 0))),
    )
    received = lax.all_to_all(
        sigma_blocks.reshape(lon_count, CAP * 2 * SIGMA_PAD, 128),
        "lon", split_axis=0, concat_axis=0, tiled=True,
    )

    table = cubic_weights(TILE)
    high = jnp.asarray(table).astype(jnp.bfloat16)
    low = (jnp.asarray(table) - high.astype(f32)).astype(jnp.bfloat16)
    per_step = 6
    nest = pl.pallas_call(
        interp_kernel,
        grid=(SIGMA // per_step,),
        in_specs=[whole((slots * 2 * SIGMA_PAD, 128))] + [whole((RIM, NCELL))] * 2,
        out_specs=pl.BlockSpec((per_step * slots, NCELL), lambda i: (i, 0)),
        out_shape=jax.ShapeDtypeStruct((SIGMA * slots, NCELL), f32),
        compiler_params=PARAMS,
        name="interpolate",
    )(received.reshape(slots * 2 * SIGMA_PAD, 128), high, low)
    nest = nest.reshape(SIGMA, slots, NCELL).transpose(1, 0, 2)
    return (
        zonal_new,
        merid_new,
        tracer_new,
        nest.reshape(1, 1, slots, SIGMA, NCELL),
    )


def solution(mesh):
    return jax.shard_map(
        per_device,
        mesh=mesh,
        in_specs=(
            P(None, "lat", "lon"),
            P(None, "lat", "lon"),
            P(None, "lat", "lon"),
            P("lat", "lon"),
            P("lat", "lon", None),
            P("lat", "lon"),
        ),
        out_specs=(
            P(None, "lat", "lon"),
            P(None, "lat", "lon"),
            P(None, "lat", "lon"),
            P("lat", "lon", None, None, None),
        ),
        check_vma=False,
    )
```

time: 294 us -> 103 us (0.35)
  the two profiles are of different devices: /device:TPU:0 before, /device:TPU:13 now
where the time goes in v1:
time: 103 us; the launch traced here: 102 us
  Pallas kernels  51.3 us (50%)
  starting transfers between devices  26.8 us (26%)
  waiting for transfers between devices  14.7 us (14%)
  local copies, waits for them, and re-layouts  7.19 us (7%)
  other arithmetic  1.25 us (1%)
    ppermute x10, starting transfers between devices, shift(): return lax.ppermute(x, axis, up if forward else [(j, i) for i, j in up])  21.5 us
    pallas_call x1, Pallas kernels, per_device(): pl.pallas_call(momentum_kernel, grid=(steps,), in_specs=[field_spec] * 3...  20.9 us
    ppermute x10, waiting for transfers between devices, shift(): return lax.ppermute(x, axis, up if forward else [(j, i) for i, j in up])  14.7 us
    pallas_call x1, Pallas kernels, per_device(): pl.pallas_call(tracer_kernel, grid=(steps,), in_specs=[field_spec] * 3 +...  9.73 us
    pallas_call x1, Pallas kernels, per_device(): pl.pallas_call(rim_kernel, in_specs=[pl.BlockSpec(memory_space=pltpu.SMEM...  7.9 us
    pallas_call x1, Pallas kernels, per_device(): pl.pallas_call(interp_kernel, grid=(SIGMA // per_step,), in_specs=[whole(...  7.47 us
    unnamed x24, local copies, waits for them, and re-layouts  6.79 us
    pallas_call x1, Pallas kernels, per_device(): pl.pallas_call(pack_kernel, grid=(steps,), in_specs=[field_spec] * 3, out...  5.36 us
  transfers between devices with their start and end apart: 11, of which 5 were waited for; matrix products, arithmetic and copies ran while one was open for 2% of the time, Pallas kernels for 20%

profile of v1, /device:TPU:13, one launch (start us, length us, event | category | flops | bytes accessed | tf_op | source)
XLA Modules:
  0.0 102.1 jit_solution(6782115179369271437)
XLA Ops:
  0.6 1.8 %copy-done = f32[75,24,384]{2,1,0:T(8,128)S(1)} copy-done((f32[75,24,384]{2,1,0:T(8,128)S(1)}, f32[75,24,384]{2,1,0:T(8,128)}, u32[]{:S(2)}) %copy-start) | copy-done | bytes 2764824
  2.4 5.4 %pack_edges.1 = (f32[240,384]{1,0:T(8,128)S(1)}, f32[240,384]{1,0:T(8,128)S(1)}, f32[3,24,128]{2,1,0:T(8,128)S(1)}, f32[3,24,128]{2,1,0:T(8,128)S(1)}) custom-call(f32[75,24,384]{2,1,0:T(8,128)S(1)} %copy-done, f32[75,24,384]{2,1,0:T(8,128)} %v_ref.5, f32[75,24,384]{2,1,0:T(8,128)} %t_ref.5), custom_call_target="tpu_custom_call" | custom-call | tf_op jit(solution)/shard_map/pack_edges/pallas_call | solution.py:279
  7.8 3.1 %collective-permute-start.2 = (f32[240,384]{1,0:T(8,128)S(1)}, f32[240,384]{1,0:T(8,128)S(1)}, u32[]{:S(2)}, u32[]{:S(2)}) collective-permute-start(f32[240,384]{1,0:T(8,128)S(1)} %get-tuple-element.18), channel_id=1, source_target_pairs={{1,0},{2,1},{3,2},{5,4},{6,5},{7,6},{9,8},{10,9},{11,10},{13,12},{... | collective-permute-start | bytes 1105928 | tf_op jit(solution)/shard_map/ppermute | solution.py:265
  10.9 2.2 %collective-permute-start.3 = (f32[240,384]{1,0:T(8,128)S(1)}, f32[240,384]{1,0:T(8,128)S(1)}, u32[]{:S(2)}, u32[]{:S(2)}) collective-permute-start(f32[240,384]{1,0:T(8,128)S(1)} %get-tuple-element.19), channel_id=1, source_target_pairs={{0,1},{1,2},{2,3},{4,5},{5,6},{6,7},{8,9},{9,10},{10,11},{12,13},{... | collective-permute-start | bytes 1105928 | tf_op jit(solution)/shard_map/ppermute | solution.py:265
  13.1 1.3 %collective-permute-start = (f32[3,24,128]{2,1,0:T(8,128)S(1)}, f32[3,24,128]{2,1,0:T(8,128)S(1)}, u32[]{:S(2)}, u32[]{:S(2)}) collective-permute-start(f32[3,24,128]{2,1,0:T(8,128)S(1)} %get-tuple-element.16), channel_id=1, source_target_pairs={{4,0},{8,4},{12,8},{16,12},{20,16},{24,20},{28,24},{0,28},{5,1},{9... | collective-permute-start | bytes 110600 | tf_op jit(solution)/shard_map/ppermute | solution.py:265
  14.4 1.2 %collective-permute-start.1 = (f32[3,24,128]{2,1,0:T(8,128)S(1)}, f32[3,24,128]{2,1,0:T(8,128)S(1)}, u32[]{:S(2)}, u32[]{:S(2)}) collective-permute-start(f32[3,24,128]{2,1,0:T(8,128)S(1)} %get-tuple-element.17), channel_id=1, source_target_pairs={{0,4},{4,8},{8,12},{12,16},{16,20},{20,24},{24,28},{28,0},{1,5},{5... | collective-permute-start | bytes 110600 | tf_op jit(solution)/shard_map/ppermute | solution.py:265
  17.5 1.6 %collective-permute-done.2.north_ref = f32[240,384]{1,0:T(8,128)S(1)} collective-permute-done((f32[240,384]{1,0:T(8,128)S(1)}, f32[240,384]{1,0:T(8,128)S(1)}, u32[]{:S(2)}, u32[]{:S(2)}) %collective-permute-start.2) | collective-permute-done | bytes 368672 | tf_op jit(solution)/shard_map/ppermute | solution.py:265
  19.1 7.8 %collective-permute-done.3.south_ref = f32[240,384]{1,0:T(8,128)S(1)} collective-permute-done((f32[240,384]{1,0:T(8,128)S(1)}, f32[240,384]{1,0:T(8,128)S(1)}, u32[]{:S(2)}, u32[]{:S(2)}) %collective-permute-start.3) | collective-permute-done | bytes 368672 | tf_op jit(solution)/shard_map/ppermute | solution.py:265
  27.0 9.7 %tracer_step.1 = (f32[75,24,384]{2,1,0:T(8,128)}, f32[3,1800,128]{2,1,0:T(8,128)S(1)}, f32[160,384]{1,0:T(8,128)S(1)}, f32[160,384]{1,0:T(8,128)S(1)}, f32[80,128]{1,0:T(8,128)S(1)}, /*index=5*/f32[80,128]{1,0:T(8,128)S(1)}) custom-call(f32[75,24,384]{2,1,0:T(8,128)} %u_ref.5, f32[75,24,384]{2,1,0:T(8,128)} %v_ref.5, f32[75,24,384]{2,1,0:T(8,128)} %t_ref.5, ...), custom_call_target="tpu_custom_call" | custom-call | tf_op jit(solution)/shard_map/tracer_step/pallas_call | solution.py:298
  36.7 1.6 %collective-permute-start.4 = (f32[80,128]{1,0:T(8,128)S(1)}, f32[80,128]{1,0:T(8,128)S(1)}, u32[]{:S(2)}, u32[]{:S(2)}) collective-permute-start(f32[80,128]{1,0:T(8,128)S(1)} %get-tuple-element.24), channel_id=1, source_target_pairs={{4,0},{8,4},{12,8},{16,12},{20,16},{24,20},{28,24},{0,28},{5,1},{9... | collective-permute-start | bytes 122888 | tf_op jit(solution)/shard_map/ppermute | solution.py:265
  38.3 1.2 %collective-permute-start.5 = (f32[80,128]{1,0:T(8,128)S(1)}, f32[80,128]{1,0:T(8,128)S(1)}, u32[]{:S(2)}, u32[]{:S(2)}) collective-permute-start(f32[80,128]{1,0:T(8,128)S(1)} %get-tuple-element.25), channel_id=1, source_target_pairs={{0,4},{4,8},{8,12},{12,16},{16,20},{20,24},{24,28},{28,0},{1,5},{5... | collective-permute-start | bytes 122888 | tf_op jit(solution)/shard_map/ppermute | solution.py:265
  39.6 1.9 %collective-permute-start.6 = (f32[160,384]{1,0:T(8,128)S(1)}, f32[160,384]{1,0:T(8,128)S(1)}, u32[]{:S(2)}, u32[]{:S(2)}) collective-permute-start(f32[160,384]{1,0:T(8,128)S(1)} %get-tuple-element.26), channel_id=1, source_target_pairs={{1,0},{2,1},{3,2},{5,4},{6,5},{7,6},{9,8},{10,9},{11,10},{13,12},{... | collective-permute-start | bytes 737288 | tf_op jit(solution)/shard_map/ppermute | solution.py:265
  41.5 3.4 %collective-permute-start.7 = (f32[160,384]{1,0:T(8,128)S(1)}, f32[160,384]{1,0:T(8,128)S(1)}, u32[]{:S(2)}, u32[]{:S(2)}) collective-permute-start(f32[160,384]{1,0:T(8,128)S(1)} %get-tuple-element.27), channel_id=1, source_target_pairs={{0,1},{1,2},{2,3},{4,5},{5,6},{6,7},{8,9},{9,10},{10,11},{12,13},{... | collective-permute-start | bytes 737288 | tf_op jit(solution)/shard_map/ppermute | solution.py:265
  45.1 3.1 %collective-permute-start.8 = (f32[2,80,128]{2,1,0:T(8,128)S(1)}, f32[2,80,128]{2,1,0:T(8,128)S(1)}, u32[]{:S(2)}, u32[]{:S(2)}) collective-permute-start(f32[2,80,128]{2,1,0:T(8,128)S(1)} %pad_maximum_fusion), channel_id=1, source_target_pairs={{1,0},{2,1},{3,2},{5,4},{6,5},{7,6},{9,8},{10,9},{11,10},{13,12},{... | collective-permute-start | bytes 245768 | tf_op jit(solution)/shard_map/ppermute | solution.py:265
  48.2 2.5 %collective-permute-start.9 = (f32[2,80,128]{2,1,0:T(8,128)S(1)}, f32[2,80,128]{2,1,0:T(8,128)S(1)}, u32[]{:S(2)}, u32[]{:S(2)}) collective-permute-start(f32[2,80,128]{2,1,0:T(8,128)S(1)} %pad_maximum_fusion), channel_id=1, source_target_pairs={{0,1},{1,2},{2,3},{4,5},{5,6},{6,7},{8,9},{9,10},{10,11},{12,13},{... | collective-permute-start | bytes 245768 | tf_op jit(solution)/shard_map/ppermute | solution.py:265
  50.8 3.4 %collective-permute-done.8.corner_n = f32[2,80,128]{2,1,0:T(8,128)S(1)} collective-permute-done((f32[2,80,128]{2,1,0:T(8,128)S(1)}, f32[2,80,128]{2,1,0:T(8,128)S(1)}, u32[]{:S(2)}, u32[]{:S(2)}) %collective-permute-start.8) | collective-permute-done | bytes 81952 | tf_op jit(solution)/shard_map/ppermute | solution.py:265
  54.2 1.3 %collective-permute-done.9.corner_s = f32[2,80,128]{2,1,0:T(8,128)S(1)} collective-permute-done((f32[2,80,128]{2,1,0:T(8,128)S(1)}, f32[2,80,128]{2,1,0:T(8,128)S(1)}, u32[]{:S(2)}, u32[]{:S(2)}) %collective-permute-start.9) | collective-permute-done | bytes 81952 | tf_op jit(solution)/shard_map/ppermute | solution.py:265
  55.5 7.9 %sigma_rims.1 = f32[16,2,32,128]{3,2,1,0:T(8,128)S(1)} custom-call(s32[16]{0:T(128)S(1)} %select_reduce_fusion.block_ref, f32[3,1800,128]{2,1,0:T(8,128)S(1)} %get-tuple-element.23.x_ref, f32[80,128]{1,0:T(8,128)S(1)} %collective-permute-done.4.east_ref, f32[80,128]{1,0:T(8,128)S(1)} %collective-permute-done.5.west_ref, ...), custom_call_target="tpu_custom_call" | custom-call | tf_op jit(solution)/shard_map/sigma_rims/pallas_call | solution.py:347
  64.2 5.2 %all-to-all-start = ((f32[8,128,128]{2,1,0:T(8,128)}), f32[8,128,128]{2,1,0:T(8,128)S(1)}, u32[]{:S(2)}, u32[]{:S(2)}) async-start(f32[8,128,128]{2,1,0:T(8,128)} %bitcast.14), calls=%async_computation | async-start | bytes 1048576 | tf_op jit(solution)/shard_map/all_to_all | solution.py:363
  69.5 1.0 copy-done.4
  71.5 20.9 %momentum_step.1 = (f32[75,24,384]{2,1,0:T(8,128)}, f32[75,24,384]{2,1,0:T(8,128)}) custom-call(f32[75,24,384]{2,1,0:T(8,128)S(1)} %copy-done.1, f32[75,24,384]{2,1,0:T(8,128)} %v_ref.5, f32[75,24,384]{2,1,0:T(8,128)} %t_ref.5, s32[24,384]{1,0:T(8,128)S(1)} %copy-done.9, f32[24,384]{1,0:T(8,128)S(1)} %broadcast_in_dim.6.coriolis_ref, ...), custom_call_target="tpu_custom_call" | custom-call | flops 41472000 | bytes 13824000 | tf_op jit(solution)/shard_map/momentum_step/pallas_call | solution.py:319
  92.4 1.1 %copy-done.7 = bf16[256,1296]{1,0:T(8,128)(2,1)S(1)} copy-done((bf16[256,1296]{1,0:T(8,128)(2,1)S(1)}, bf16[256,1296]{1,0:T(8,128)(2,1)}, u32[]{:S(2)}) %copy-start.7) | copy-done | bytes 663576
  93.5 1.1 %copy-done.8 = bf16[256,1296]{1,0:T(8,128)(2,1)S(1)} copy-done((bf16[256,1296]{1,0:T(8,128)(2,1)S(1)}, bf16[256,1296]{1,0:T(8,128)(2,1)}, u32[]{:S(2)}) %copy-start.8) | copy-done | bytes 663576
  94.6 7.5 %interpolate.1 = f32[480,1296]{1,0:T(8,128)} custom-call(f32[1024,128]{1,0:T(8,128)S(1)} %bitcast.13, bf16[256,1296]{1,0:T(8,128)(2,1)S(1)} %copy-done.7, bf16[256,1296]{1,0:T(8,128)(2,1)S(1)} %copy-done.8), custom_call_target="tpu_custom_call" | custom-call | tf_op jit(solution)/shard_map/interpolate/pallas_call | solution.py:372
  (42 shorter events, 4.1 us)
Async XLA Ops:
  0.6 1.8 %copy-start = (f32[75,24,384]{2,1,0:T(8,128)S(1)}, f32[75,24,384]{2,1,0:T(8,128)}, u32[]{:S(2)}) copy-start(f32[75,24,384]{2,1,0:T(8,128)} %u_ref.5) | copy-start | bytes 8294404
  2.4 13.2 %copy-start.11 = (s32[2,32]{1,0:T(2,128)S(1)}, s32[2,32]{1,0:T(2,128)}, u32[]{:S(2)}) copy-start(s32[2,32]{1,0:T(2,128)} %param.12) | copy-start | bytes 772
  2.4 13.5 %copy-start.10 = (s32[2,32,31]{1,0,2:T(2,128)S(1)}, s32[2,32,31]{1,0,2:T(2,128)}, u32[]{:S(2)}) copy-start(s32[2,32,31]{1,0,2:T(2,128)} %param.11) | copy-start | bytes 23812
  2.4 24.6 %copy-start.9 = (s32[24,384]{1,0:T(8,128)S(1)}, s32[24,384]{1,0:T(8,128)}, u32[]{:S(2)}) copy-start(s32[24,384]{1,0:T(8,128)} %mask_ref.3) | copy-start | bytes 110596
  7.8 11.3 %collective-permute-start.2 = (f32[240,384]{1,0:T(8,128)S(1)}, f32[240,384]{1,0:T(8,128)S(1)}, u32[]{:S(2)}, u32[]{:S(2)}) collective-permute-start(f32[240,384]{1,0:T(8,128)S(1)} %get-tuple-element.18), channel_id=1, source_target_pairs={{1,0},{2,1},{3,2},{5,4},{6,5},{7,6},{9,8},{10,9},{11,10},{13,12},{... | collective-permute-start | bytes 1105928 | tf_op jit(solution)/shard_map/ppermute | solution.py:265
  10.9 16.1 %collective-permute-start.3 = (f32[240,384]{1,0:T(8,128)S(1)}, f32[240,384]{1,0:T(8,128)S(1)}, u32[]{:S(2)}, u32[]{:S(2)}) collective-permute-start(f32[240,384]{1,0:T(8,128)S(1)} %get-tuple-element.19), channel_id=1, source_target_pairs={{0,1},{1,2},{2,3},{4,5},{5,6},{6,7},{8,9},{9,10},{10,11},{12,13},{... | collective-permute-start | bytes 1105928 | tf_op jit(solution)/shard_map/ppermute | solution.py:265
  13.1 4.4 %collective-permute-start = (f32[3,24,128]{2,1,0:T(8,128)S(1)}, f32[3,24,128]{2,1,0:T(8,128)S(1)}, u32[]{:S(2)}, u32[]{:S(2)}) collective-permute-start(f32[3,24,128]{2,1,0:T(8,128)S(1)} %get-tuple-element.16), channel_id=1, source_target_pairs={{4,0},{8,4},{12,8},{16,12},{20,16},{24,20},{28,24},{0,28},{5,1},{9... | collective-permute-start | bytes 110600 | tf_op jit(solution)/shard_map/ppermute | solution.py:265
  14.4 3.1 %collective-permute-start.1 = (f32[3,24,128]{2,1,0:T(8,128)S(1)}, f32[3,24,128]{2,1,0:T(8,128)S(1)}, u32[]{:S(2)}, u32[]{:S(2)}) collective-permute-start(f32[3,24,128]{2,1,0:T(8,128)S(1)} %get-tuple-element.17), channel_id=1, source_target_pairs={{0,4},{4,8},{8,12},{12,16},{16,20},{20,24},{24,28},{28,0},{1,5},{5... | collective-permute-start | bytes 110600 | tf_op jit(solution)/shard_map/ppermute | solution.py:265
  19.1 17.6 %copy-start.3 = (f32[240,384]{1,0:T(8,128)}, f32[240,384]{1,0:T(8,128)S(1)}, u32[]{:S(2)}) copy-start(f32[240,384]{1,0:T(8,128)S(1)} %collective-permute-done.2.north_ref) | copy-start | bytes 1105924
  27.0 9.7 %copy-start.5 = (f32[240,384]{1,0:T(8,128)}, f32[240,384]{1,0:T(8,128)S(1)}, u32[]{:S(2)}) copy-start(f32[240,384]{1,0:T(8,128)S(1)} %collective-permute-done.3.south_ref) | copy-start | bytes 1105924
  36.7 8.4 %collective-permute-start.4 = (f32[80,128]{1,0:T(8,128)S(1)}, f32[80,128]{1,0:T(8,128)S(1)}, u32[]{:S(2)}, u32[]{:S(2)}) collective-permute-start(f32[80,128]{1,0:T(8,128)S(1)} %get-tuple-element.24), channel_id=1, source_target_pairs={{4,0},{8,4},{12,8},{16,12},{20,16},{24,20},{28,24},{0,28},{5,1},{9... | collective-permute-start | bytes 122888 | tf_op jit(solution)/shard_map/ppermute | solution.py:265
  38.3 6.8 %collective-permute-start.5 = (f32[80,128]{1,0:T(8,128)S(1)}, f32[80,128]{1,0:T(8,128)S(1)}, u32[]{:S(2)}, u32[]{:S(2)}) collective-permute-start(f32[80,128]{1,0:T(8,128)S(1)} %get-tuple-element.25), channel_id=1, source_target_pairs={{0,4},{4,8},{8,12},{12,16},{16,20},{20,24},{24,28},{28,0},{1,5},{5... | collective-permute-start | bytes 122888 | tf_op jit(solution)/shard_map/ppermute | solution.py:265
  39.6 15.9 %collective-permute-start.6 = (f32[160,384]{1,0:T(8,128)S(1)}, f32[160,384]{1,0:T(8,128)S(1)}, u32[]{:S(2)}, u32[]{:S(2)}) collective-permute-start(f32[160,384]{1,0:T(8,128)S(1)} %get-tuple-element.26), channel_id=1, source_target_pairs={{1,0},{2,1},{3,2},{5,4},{6,5},{7,6},{9,8},{10,9},{11,10},{13,12},{... | collective-permute-start | bytes 737288 | tf_op jit(solution)/shard_map/ppermute | solution.py:265
  41.5 14.0 %collective-permute-start.7 = (f32[160,384]{1,0:T(8,128)S(1)}, f32[160,384]{1,0:T(8,128)S(1)}, u32[]{:S(2)}, u32[]{:S(2)}) collective-permute-start(f32[160,384]{1,0:T(8,128)S(1)} %get-tuple-element.27), channel_id=1, source_target_pairs={{0,1},{1,2},{2,3},{4,5},{5,6},{6,7},{8,9},{9,10},{10,11},{12,13},{... | collective-permute-start | bytes 737288 | tf_op jit(solution)/shard_map/ppermute | solution.py:265
  45.1 24.5 %copy-start.1 = (f32[75,24,384]{2,1,0:T(8,128)S(1)}, f32[75,24,384]{2,1,0:T(8,128)}, u32[]{:S(2)}) copy-start(f32[75,24,384]{2,1,0:T(8,128)} %u_ref.5) | copy-start | bytes 8294404
  45.1 9.1 %collective-permute-start.8 = (f32[2,80,128]{2,1,0:T(8,128)S(1)}, f32[2,80,128]{2,1,0:T(8,128)S(1)}, u32[]{:S(2)}, u32[]{:S(2)}) collective-permute-start(f32[2,80,128]{2,1,0:T(8,128)S(1)} %pad_maximum_fusion), channel_id=1, source_target_pairs={{1,0},{2,1},{3,2},{5,4},{6,5},{7,6},{9,8},{10,9},{11,10},{13,12},{... | collective-permute-start | bytes 245768 | tf_op jit(solution)/shard_map/ppermute | solution.py:265
  48.2 7.3 %collective-permute-start.9 = (f32[2,80,128]{2,1,0:T(8,128)S(1)}, f32[2,80,128]{2,1,0:T(8,128)S(1)}, u32[]{:S(2)}, u32[]{:S(2)}) collective-permute-start(f32[2,80,128]{2,1,0:T(8,128)S(1)} %pad_maximum_fusion), channel_id=1, source_target_pairs={{0,1},{1,2},{2,3},{4,5},{5,6},{6,7},{8,9},{9,10},{10,11},{12,13},{... | collective-permute-start | bytes 245768 | tf_op jit(solution)/shard_map/ppermute | solution.py:265
  63.4 0.8 copy-start.2
  64.2 28.2 %all-to-all-start = ((f32[8,128,128]{2,1,0:T(8,128)}), f32[8,128,128]{2,1,0:T(8,128)S(1)}, u32[]{:S(2)}, u32[]{:S(2)}) async-start(f32[8,128,128]{2,1,0:T(8,128)} %bitcast.14), calls=%async_computation | async-start | bytes 1048576 | tf_op jit(solution)/shard_map/all_to_all | solution.py:363
  69.5 1.0 copy-start.4
  70.5 1.0 copy-start.6
  92.4 1.1 %copy-start.7 = (bf16[256,1296]{1,0:T(8,128)(2,1)S(1)}, bf16[256,1296]{1,0:T(8,128)(2,1)}, u32[]{:S(2)}) copy-start(bf16[256,1296]{1,0:T(8,128)(2,1)} %constant.30.high_ref) | copy-start | bytes 1990660
  93.5 1.1 %copy-start.8 = (bf16[256,1296]{1,0:T(8,128)(2,1)S(1)}, bf16[256,1296]{1,0:T(8,128)(2,1)}, u32[]{:S(2)}) copy-start(bf16[256,1296]{1,0:T(8,128)(2,1)} %constant.33.low_ref) | copy-start | bytes 1990660

commit v2 on v1

--- a/solution.py
+++ b/solution.py
@@ -90,16 +90,24 @@
 
 def neighbours(x, f, k, east_ref, west_ref, north_ref, south_ref):
     rows, cols = x.shape
-    col = lax.broadcasted_iota(jnp.int32, (rows, cols), 1)
-    row = lax.broadcasted_iota(jnp.int32, (rows, cols), 0)
+    lane = lax.broadcasted_iota(jnp.int32, (rows, 128), 1)
+    row = lax.broadcasted_iota(jnp.int32, (8, cols), 0)
     e_col = pltpu.roll(east_ref[f], 127 - k, axis=1)[:, 127:128]
     w_col = pltpu.roll(west_ref[f], 127 - k, axis=1)[:, 127:128]
     n_row = north_ref[pl.ds(f * LEVEL_PAD + k, 1), :]
     s_row = south_ref[pl.ds(f * LEVEL_PAD + k, 1), :]
-    east = jnp.where(col == cols - 1, e_col, pltpu.roll(x, cols - 1, axis=1))
-    west = jnp.where(col == 0, w_col, pltpu.roll(x, 1, axis=1))
-    north = jnp.where(row == rows - 1, n_row, pltpu.roll(x, rows - 1, axis=0))
-    south = jnp.where(row == 0, s_row, pltpu.roll(x, 1, axis=0))
+    east = pltpu.roll(x, cols - 1, axis=1)
+    tail = jnp.where(lane == 127, e_col, east[:, cols - 128 :])
+    east = jnp.concatenate([east[:, : cols - 128], tail], axis=1)
+    west = pltpu.roll(x, 1, axis=1)
+    head = jnp.where(lane == 0, w_col, west[:, :128])
+    west = jnp.concatenate([head, west[:, 128:]], axis=1)
+    north = pltpu.roll(x, rows - 1, axis=0)
+    tail = jnp.where(row == 7, n_row, north[rows - 8 :])
+    north = jnp.concatenate([north[: rows - 8], tail], axis=0)
+    south = pltpu.roll(x, 1, axis=0)
+    head = jnp.where(row == 0, s_row, south[:8])
+    south = jnp.concatenate([head, south[8:]], axis=0)
     return 0.5 * (east - west), 0.5 * (north - south), east + west + north + south - 4.0 * x
 
 
@@ -259,10 +267,104 @@
         )
 
 
-def shift(x, axis, wrap, forward):
-    count = lax.axis_size(axis)
-    up = [(i, (i + 1) % count) for i in range(count if wrap else count - 1)]
-    return lax.ppermute(x, axis, up if forward else [(j, i) for i, j in up])
+def exchange_kernel(
+    corners, first_row, last_row, first_col, last_col, north, south, east, west, *rest
+):
+    corner_n, corner_s = rest[:2] if corners else (None, None)
+    send, recv = rest[-2:]
+    lon_count, lat_count = lax.axis_size("lon"), lax.axis_size("lat")
+    lon, lat = lax.axis_index("lon"), lax.axis_index("lat")
+    right = (lax.rem(lon + 1, lon_count), lat)
+    left = (lax.rem(lon + lon_count - 1, lon_count), lat)
+    up = (lon, lax.rem(lat + 1, lat_count))
+    down = (lon, lax.rem(lat + lat_count - 1, lat_count))
+    mesh_id = pl.DeviceIdType.MESH
+    has_up, has_down = lat < lat_count - 1, lat > 0
+    barrier = pltpu.get_barrier_semaphore()
+
+    def greet(device):
+        pl.semaphore_signal(barrier, inc=1, device_id=device, device_id_type=mesh_id)
+
+    greet(left)
+    greet(right)
+    pl.when(has_up)(lambda: greet(up))
+    pl.when(has_down)(lambda: greet(down))
+    pl.semaphore_wait(barrier, 2 + has_up.astype(jnp.int32) + has_down.astype(jnp.int32))
+
+    def copy(n, src, dst, device):
+        return pltpu.make_async_remote_copy(
+            src_ref=src, dst_ref=dst, send_sem=send.at[n], recv_sem=recv.at[n],
+            device_id=device, device_id_type=mesh_id,
+        )
+
+    to_west = copy(0, first_col, east, left)
+    to_east = copy(1, last_col, west, right)
+    to_down = [copy(2, first_row, north, down)]
+    to_up = [copy(3, last_row, south, up)]
+    to_west.start()
+    to_east.start()
+    pl.when(has_down)(lambda: to_down[0].start())
+    pl.when(has_up)(lambda: to_up[0].start())
+    to_west.wait()
+    to_east.wait()
+    if corners:
+        for n, ref in enumerate((east, west)):
+            to_down.append(copy(4 + n, ref, corner_n.at[n], down))
+            to_up.append(copy(6 + n, ref, corner_s.at[n], up))
+
+    @pl.when(has_down)
+    def _():
+        for c in to_down[1:]:
+            c.start()
+
+    @pl.when(has_up)
+    def _():
+        for c in to_up[1:]:
+            c.start()
+
+    @pl.when(has_down)
+    def _():
+        for c in to_down:
+            c.wait_send()
+        for c in to_up:
+            c.wait_recv()
+
+    @pl.when(has_up)
+    def _():
+        for c in to_up:
+            c.wait_send()
+        for c in to_down:
+            c.wait_recv()
+
+    @pl.when(jnp.logical_not(has_up))
+    def _():
+        north[...] = jnp.zeros_like(north)
+        if corners:
+            corner_n[...] = jnp.zeros_like(corner_n)
+
+    @pl.when(jnp.logical_not(has_down))
+    def _():
+        south[...] = jnp.zeros_like(south)
+        if corners:
+            corner_s[...] = jnp.zeros_like(corner_s)
+
+
+def exchange(first_row, last_row, first_col, last_col, corners):
+    row, col = first_row.shape, first_col.shape
+    shapes = [row, row, col, col] + ([(2,) + col] * 2 if corners else [])
+    vmem = pl.BlockSpec(memory_space=pltpu.VMEM)
+    sems = 8 if corners else 4
+    return pl.pallas_call(
+        functools.partial(exchange_kernel, corners),
+        in_specs=[vmem] * 4,
+        out_specs=[vmem] * len(shapes),
+        out_shape=[jax.ShapeDtypeStruct(s, jnp.float32) for s in shapes],
+        scratch_shapes=[pltpu.SemaphoreType.DMA((sems,)), pltpu.SemaphoreType.DMA((sems,))],
+        compiler_params=pltpu.CompilerParams(
+            collective_id=1 if corners else 0, has_side_effects=True
+        ),
+        name="exchange_margins" if corners else "exchange_edges",
+    )(first_row, last_row, first_col, last_col)
 
 
 def per_device(zonal_velocity, meridional_velocity, tracer, land_mask, remap_bounds, nest_owner):
@@ -286,10 +388,7 @@
         compiler_params=PARAMS,
         name="pack_edges",
     )(*fields)
-    north = shift(first_row, "lat", False, False)
-    south = shift(last_row, "lat", False, True)
-    east = shift(first_col, "lon", True, False)
-    west = shift(last_col, "lon", True, True)
+    north, south, east, west = exchange(first_row, last_row, first_col, last_col, False)
     halos = (east, west, north, south)
     halo_specs = [whole(col_shape)] * 2 + [whole(row_shape)] * 2
 
@@ -306,13 +405,9 @@
         compiler_params=PARAMS,
         name="tracer_step",
     )(*fields, land_mask, *halos)
-    east_margin = shift(west_cols, "lon", True, False)
-    west_margin = shift(east_cols, "lon", True, True)
-    north_margin = shift(low_rows, "lat", False, False)
-    south_margin = shift(high_rows, "lat", False, True)
-    sides = jnp.stack([east_margin, west_margin])
-    corner_n = shift(sides, "lat", False, False)
-    corner_s = shift(sides, "lat", False, True)
+    north_margin, south_margin, east_margin, west_margin, corner_n, corner_s = exchange(
+        low_rows, high_rows, west_cols, east_cols, True
+    )
 
     row_index = lax.axis_index("lat") * rows + jnp.arange(rows, dtype=jnp.int32)
     coriolis = jnp.broadcast_to(coriolis_rows(row_index), (rows, cols))

time: 103 us -> 126 us (1.22)
  Pallas kernels: 51.3 us -> 91.2 us
  starting transfers between devices: 26.8 us -> 5.84 us
  local copies, waits for them, and re-layouts: 7.19 us -> 26.1 us
  waiting for transfers between devices: 14.7 us -> 0.01 us
    pallas_call x0 -> x2, Pallas kernels: none -> 40 us  [exchange(): pl.pallas_call(functools.partial(exchange_kernel, corners), in_specs=[vme...]
    ppermute x10 -> x0, starting transfers between devices: 21.5 us -> none  [shift(): return lax.ppermute(x, axis, up if forward else [(j, i) for i, j in up])]
    unnamed x24 -> x60, local copies, waits for them, and re-layouts: 6.79 us -> 24.3 us
    ppermute x10 -> x0, waiting for transfers between devices: 14.7 us -> none  [shift(): return lax.ppermute(x, axis, up if forward else [(j, i) for i, j in up])]
  transfers between devices with their start and end apart: 11 -> 1, of which waited for: 5 -> 0; matrix products, arithmetic and copies ran while one was open for 2% -> 0% of each run, Pallas kernels for 20% -> 17%
where the time goes in v2:
time: 126 us; the launch traced here: 125 us
  Pallas kernels  91.2 us (72%)
  local copies, waits for them, and re-layouts  26.1 us (21%)
  starting transfers between devices  5.84 us (5%)
    pallas_call x2, Pallas kernels, exchange(): pl.pallas_call(functools.partial(exchange_kernel, corners), in_specs=[vme...  40 us
    unnamed x60, local copies, waits for them, and re-layouts  24.3 us
    pallas_call x1, Pallas kernels, per_device(): pl.pallas_call(momentum_kernel, grid=(steps,), in_specs=[field_spec] * 3...  20.9 us
    pallas_call x1, Pallas kernels, per_device(): pl.pallas_call(tracer_kernel, grid=(steps,), in_specs=[field_spec] * 3 +...  9.6 us
    pallas_call x1, Pallas kernels, per_device(): pl.pallas_call(rim_kernel, in_specs=[pl.BlockSpec(memory_space=pltpu.SMEM...  7.9 us
    pallas_call x1, Pallas kernels, per_device(): pl.pallas_call(interp_kernel, grid=(SIGMA // per_step,), in_specs=[whole(...  7.47 us
    all_to_all x1, starting transfers between devices, per_device(): lax.all_to_all(sigma_blocks.reshape(lon_count, CAP * 2 * SIGMA_PAD, 128),...  5.84 us
    pallas_call x1, Pallas kernels, per_device(): pl.pallas_call(pack_kernel, grid=(steps,), in_specs=[field_spec] * 3, out...  5.33 us
  transfers between devices with their start and end apart: 1, of which 0 were waited for; matrix products, arithmetic and copies ran while one was open for 0% of the time, Pallas kernels for 17%

profile of v2, /device:TPU:13, one launch (start us, length us, event | category | flops | bytes accessed | tf_op | source)
XLA Modules:
  0.0 125.2 jit_solution(16783791147630078671)
XLA Ops:
  1.6 0.8 mul.66
  3.6 1.8 %copy-done = f32[75,24,384]{2,1,0:T(8,128)S(1)} copy-done((f32[75,24,384]{2,1,0:T(8,128)S(1)}, f32[75,24,384]{2,1,0:T(8,128)}, u32[]{:S(2)}) %copy-start) | copy-done | bytes 2764824
  5.4 5.3 %pack_edges.1 = (f32[240,384]{1,0:T(8,128)S(1)}, f32[240,384]{1,0:T(8,128)S(1)}, f32[3,24,128]{2,1,0:T(8,128)S(1)}, f32[3,24,128]{2,1,0:T(8,128)S(1)}) custom-call(f32[75,24,384]{2,1,0:T(8,128)S(1)} %copy-done, f32[75,24,384]{2,1,0:T(8,128)} %v_ref.5, f32[75,24,384]{2,1,0:T(8,128)} %t_ref.5), custom_call_target="tpu_custom_call" | custom-call | tf_op jit(solution)/shard_map/pack_edges/pallas_call | solution.py:381
  13.5 21.7 %exchange_edges.1 = (f32[240,384]{1,0:T(8,128)}, f32[240,384]{1,0:T(8,128)}, f32[3,24,128]{2,1,0:T(8,128)}, f32[3,24,128]{2,1,0:T(8,128)}) custom-call(f32[240,384]{1,0:T(8,128)} %copy-done.11, f32[240,384]{1,0:T(8,128)} %copy-done.12, f32[3,24,128]{2,1,0:T(8,128)} %copy-done.28, f32[3,24,128]{2,1,0:T(8,128)} %copy-done.29), custom_call_target="tpu_custom_call" | custom-call | tf_op jit(solution)/shard_map/exchange_edges/pallas_call | solution.py:357
  35.2 1.0 copy-done.5
  36.2 1.0 copy-done.7
  38.7 9.6 %tracer_step.1 = (f32[75,24,384]{2,1,0:T(8,128)}, f32[3,1800,128]{2,1,0:T(8,128)S(1)}, f32[160,384]{1,0:T(8,128)S(1)}, f32[160,384]{1,0:T(8,128)S(1)}, f32[80,128]{1,0:T(8,128)S(1)}, /*index=5*/f32[80,128]{1,0:T(8,128)S(1)}) custom-call(f32[75,24,384]{2,1,0:T(8,128)} %u_ref.5, f32[75,24,384]{2,1,0:T(8,128)} %v_ref.5, f32[75,24,384]{2,1,0:T(8,128)} %t_ref.5, ...), custom_call_target="tpu_custom_call" | custom-call | tf_op jit(solution)/shard_map/tracer_step/pallas_call | solution.py:397
  48.3 1.5 %copy-done.2 = f32[3,1800,128]{2,1,0:T(8,128)} copy-done((f32[3,1800,128]{2,1,0:T(8,128)}, f32[3,1800,128]{2,1,0:T(8,128)S(1)}, u32[]{:S(2)}) %copy-start.2) | copy-done | bytes 2764824
  52.5 18.3 %exchange_margins.1 = (f32[160,384]{1,0:T(8,128)}, f32[160,384]{1,0:T(8,128)}, f32[80,128]{1,0:T(8,128)}, f32[80,128]{1,0:T(8,128)}, f32[2,80,128]{2,1,0:T(8,128)}, /*index=5*/f32[2,80,128]{2,1,0:T(8,128)}) custom-call(f32[160,384]{1,0:T(8,128)} %copy-done.13, f32[160,384]{1,0:T(8,128)} %copy-done.14, f32[80,128]{1,0:T(8,128)} %copy-done.24, ...), custom_call_target="tpu_custom_call" | custom-call | tf_op jit(solution)/shard_map/exchange_margins/pallas_call | solution.py:357
  70.8 1.9 %copy-done.3 = f32[3,1800,128]{2,1,0:T(8,128)S(1)} copy-done((f32[3,1800,128]{2,1,0:T(8,128)S(1)}, f32[3,1800,128]{2,1,0:T(8,128)}, u32[]{:S(2)}) %copy-start.3) | copy-done | bytes 2764824
  72.7 0.9 copy-done.15
  73.7 0.9 copy-done.16
  74.6 0.9 copy-done.22
  75.5 0.9 copy-done.23
  76.4 0.8 copy-done.26
  78.0 7.9 %sigma_rims.1 = f32[16,2,32,128]{3,2,1,0:T(8,128)S(1)} custom-call(s32[16]{0:T(128)S(1)} %select_reduce_fusion.block_ref, f32[3,1800,128]{2,1,0:T(8,128)S(1)} %copy-done.3, f32[80,128]{1,0:T(8,128)S(1)} %copy-done.26, f32[80,128]{1,0:T(8,128)S(1)} %copy-done.27, f32[160,384]{1,0:T(8,128)S(1)} %copy-done.15, f32[160,384]{1,0:T(8,128)S(1)} %copy-done.16, ...), custom_call_target="tpu_custom_call" | custom-call | tf_op jit(solution)/shard_map/sigma_rims/pallas_call | solution.py:442
  85.9 0.8 copy-done.4
  86.7 5.8 %all-to-all-start = ((f32[8,128,128]{2,1,0:T(8,128)}), f32[8,128,128]{2,1,0:T(8,128)S(1)}, u32[]{:S(2)}, u32[]{:S(2)}) async-start(f32[8,128,128]{2,1,0:T(8,128)} %bitcast.12), calls=%async_computation | async-start | bytes 1048576 | tf_op jit(solution)/shard_map/all_to_all | solution.py:458
  92.6 1.0 copy-done.6
  93.6 1.0 copy-done.8
  94.6 20.9 %momentum_step.1 = (f32[75,24,384]{2,1,0:T(8,128)}, f32[75,24,384]{2,1,0:T(8,128)}) custom-call(f32[75,24,384]{2,1,0:T(8,128)S(1)} %copy-done.1, f32[75,24,384]{2,1,0:T(8,128)} %v_ref.5, f32[75,24,384]{2,1,0:T(8,128)} %t_ref.5, s32[24,384]{1,0:T(8,128)S(1)} %copy-done.17, f32[24,384]{1,0:T(8,128)S(1)} %broadcast_in_dim.6.coriolis_ref, ...), custom_call_target="tpu_custom_call" | custom-call | flops 41472000 | bytes 13824000 | tf_op jit(solution)/shard_map/momentum_step/pallas_call | solution.py:414
  115.5 1.1 copy-done.9
  116.6 1.1 copy-done.10
  117.7 7.5 %interpolate.1 = f32[480,1296]{1,0:T(8,128)} custom-call(f32[1024,128]{1,0:T(8,128)S(1)} %bitcast.11, bf16[256,1296]{1,0:T(8,128)(2,1)S(1)} %copy-done.9, bf16[256,1296]{1,0:T(8,128)(2,1)S(1)} %copy-done.10), custom_call_target="tpu_custom_call" | custom-call | tf_op jit(solution)/shard_map/interpolate/pallas_call | solution.py:467
  (59 shorter events, 9.9 us)
Async XLA Ops:
  3.6 1.8 %copy-start = (f32[75,24,384]{2,1,0:T(8,128)S(1)}, f32[75,24,384]{2,1,0:T(8,128)}, u32[]{:S(2)}) copy-start(f32[75,24,384]{2,1,0:T(8,128)} %u_ref.5) | copy-start | bytes 8294404
  5.4 29.8 %copy-start.17 = (s32[24,384]{1,0:T(8,128)S(1)}, s32[24,384]{1,0:T(8,128)}, u32[]{:S(2)}) copy-start(s32[24,384]{1,0:T(8,128)} %mask_ref.3) | copy-start | bytes 110596
  10.7 0.7 copy-start.11
  35.2 1.0 copy-start.5
  36.2 1.0 copy-start.7
  37.2 0.8 copy-start.18
  37.9 0.8 copy-start.20
  48.3 1.5 %copy-start.2 = (f32[3,1800,128]{2,1,0:T(8,128)}, f32[3,1800,128]{2,1,0:T(8,128)S(1)}, u32[]{:S(2)}) copy-start(f32[3,1800,128]{2,1,0:T(8,128)S(1)} %get-tuple-element.37.x_ref) | copy-start | bytes 8294404
  52.5 40.2 %copy-start.19 = (f32[3,24,128]{2,1,0:T(8,128)S(1)}, f32[3,24,128]{2,1,0:T(8,128)}, u32[]{:S(2)}) copy-start(f32[3,24,128]{2,1,0:T(8,128)} %get-tuple-element.30.east_ref) | copy-start | bytes 110596
  52.5 40.2 %copy-start.21 = (f32[3,24,128]{2,1,0:T(8,128)S(1)}, f32[3,24,128]{2,1,0:T(8,128)}, u32[]{:S(2)}) copy-start(f32[3,24,128]{2,1,0:T(8,128)} %get-tuple-element.31.west_ref) | copy-start | bytes 110596
  70.8 21.8 %copy-start.1 = (f32[75,24,384]{2,1,0:T(8,128)S(1)}, f32[75,24,384]{2,1,0:T(8,128)}, u32[]{:S(2)}) copy-start(f32[75,24,384]{2,1,0:T(8,128)} %u_ref.5) | copy-start | bytes 8294404
  70.8 1.9 %copy-start.3 = (f32[3,1800,128]{2,1,0:T(8,128)S(1)}, f32[3,1800,128]{2,1,0:T(8,128)}, u32[]{:S(2)}) copy-start(f32[3,1800,128]{2,1,0:T(8,128)} %copy-done.2) | copy-start | bytes 8294404
  72.7 0.9 copy-start.15
  73.7 0.9 copy-start.16
  74.6 0.9 copy-start.22
  75.5 0.9 copy-start.23
  76.4 0.8 copy-start.26
  77.2 0.8 copy-start.27
  85.9 0.8 copy-start.4
  86.7 28.9 %all-to-all-start = ((f32[8,128,128]{2,1,0:T(8,128)}), f32[8,128,128]{2,1,0:T(8,128)S(1)}, u32[]{:S(2)}, u32[]{:S(2)}) async-start(f32[8,128,128]{2,1,0:T(8,128)} %bitcast.12), calls=%async_computation | async-start | bytes 1048576 | tf_op jit(solution)/shard_map/all_to_all | solution.py:458
  92.6 1.0 copy-start.6
  93.6 1.0 copy-start.8
  115.5 1.1 copy-start.9
  116.6 1.1 copy-start.10
  (7 other events, 4.6 us)

commit v3 on v1

--- a/solution.py
+++ b/solution.py
@@ -171,7 +171,7 @@
 
 
 def rim_kernel(
-    block_ref, x_ref, east_ref, west_ref, north_ref, south_ref, corner_n, corner_s, inside_ref,
+    block_ref, x_ref, east_ref, west_ref, north_ref, south_ref, inside_ref,
     out_ref, wide, rim,
 ):
     levels = inside_ref.shape[2]
@@ -190,15 +190,16 @@
         wide[r + 2, 0:levels, cols : cols + 128] = side(
             east_ref[0:levels, :], west_ref[0:levels, :], r
         )
+    second_set = slice(LEVEL_PAD, LEVEL_PAD + levels)
     for j in range(2):
         at = slice(j * LEVEL_PAD, j * LEVEL_PAD + levels)
-        wide[j, 0:levels, 0:cols] = south_ref[at, :]
+        wide[j, 0:levels, 0:cols] = south_ref[at, 0:cols]
         wide[j, 0:levels, cols : cols + 128] = side(
-            corner_s[0, 0:levels, :], corner_s[1, 0:levels, :], rows - 2 + j
-        )
-        wide[rows + 2 + j, 0:levels, 0:cols] = north_ref[at, :]
+            south_ref[0:levels, cols:], south_ref[second_set, cols:], rows - 2 + j
+        )
+        wide[rows + 2 + j, 0:levels, 0:cols] = north_ref[at, 0:cols]
         wide[rows + 2 + j, 0:levels, cols : cols + 128] = side(
-            corner_n[0, 0:levels, :], corner_n[1, 0:levels, :], j
+            north_ref[0:levels, cols:], north_ref[second_set, cols:], j
         )
 
     ring = cols + 128
@@ -308,11 +309,9 @@
     )(*fields, land_mask, *halos)
     east_margin = shift(west_cols, "lon", True, False)
     west_margin = shift(east_cols, "lon", True, True)
-    north_margin = shift(low_rows, "lat", False, False)
-    south_margin = shift(high_rows, "lat", False, True)
-    sides = jnp.stack([east_margin, west_margin])
-    corner_n = shift(sides, "lat", False, False)
-    corner_s = shift(sides, "lat", False, True)
+    sides = jnp.concatenate([east_margin, west_margin], axis=0)
+    north_margin = shift(jnp.concatenate([low_rows, sides], axis=1), "lat", False, False)
+    south_margin = shift(jnp.concatenate([high_rows, sides], axis=1), "lat", False, True)
 
     row_index = lax.axis_index("lat") * rows + jnp.arange(rows, dtype=jnp.int32)
     coriolis = jnp.broadcast_to(coriolis_rows(row_index), (rows, cols))
@@ -346,7 +345,7 @@
     vmem = pl.BlockSpec(memory_space=pltpu.VMEM)
     sigma_blocks = pl.pallas_call(
         rim_kernel,
-        in_specs=[pl.BlockSpec(memory_space=pltpu.SMEM)] + [vmem] * 8,
+        in_specs=[pl.BlockSpec(memory_space=pltpu.SMEM)] + [vmem] * 6,
         out_specs=vmem,
         out_shape=jax.ShapeDtypeStruct((slots, 2, SIGMA_PAD, 128), f32),
         scratch_shapes=[
@@ -357,7 +356,6 @@
         name="sigma_rims",
     )(
         block_of, tiles, east_margin, west_margin, north_margin, south_margin,
-        corner_n, corner_s,
         jnp.pad(inside, ((0, 0), (0, SIGMA_PAD - inside.shape[1]), (0, 0))),
     )
     received = lax.all_to_all(

time: 103 us -> 107 us (1.039)
  waiting for transfers between devices: 14.7 us -> 22.3 us
  starting transfers between devices: 26.8 us -> 22.3 us
    ppermute x10 -> x8, waiting for transfers between devices: 14.7 us -> 22.3 us  [shift(): return lax.ppermute(x, axis, up if forward else [(j, i) for i, j in up])]
    ppermute x10 -> x8, starting transfers between devices: 21.5 us -> 15.9 us  [shift(): return lax.ppermute(x, axis, up if forward else [(j, i) for i, j in up])]
    all_to_all x1, starting transfers between devices: 5.25 us -> 6.41 us  [per_device(): lax.all_to_all(sigma_blocks.reshape(lon_count, CAP * 2 * SIGMA_PAD, 128),...]
    unnamed x24 -> x25, local copies, waits for them, and re-layouts: 6.79 us -> 6.79 us
  transfers between devices with their start and end apart: 11 -> 9, of which waited for: 5 -> 6; matrix products, arithmetic and copies ran while one was open for 2% -> 2% of each run, Pallas kernels for 20% -> 20%
where the time goes in v3:
time: 107 us; the launch traced here: 105 us
  Pallas kernels  51.3 us (48%)
  starting transfers between devices  22.3 us (21%)
  waiting for transfers between devices  22.3 us (21%)
  local copies, waits for them, and re-layouts  7.19 us (7%)
  other arithmetic  1.29 us (1%)
    ppermute x8, waiting for transfers between devices, shift(): return lax.ppermute(x, axis, up if forward else [(j, i) for i, j in up])  22.3 us
    pallas_call x1, Pallas kernels, per_device(): pl.pallas_call(momentum_kernel, grid=(steps,), in_specs=[field_spec] * 3...  20.9 us
    ppermute x8, starting transfers between devices, shift(): return lax.ppermute(x, axis, up if forward else [(j, i) for i, j in up])  15.9 us
    pallas_call x1, Pallas kernels, per_device(): pl.pallas_call(tracer_kernel, grid=(steps,), in_specs=[field_spec] * 3 +...  9.73 us
    pallas_call x1, Pallas kernels, per_device(): pl.pallas_call(rim_kernel, in_specs=[pl.BlockSpec(memory_space=pltpu.SMEM...  7.9 us
    pallas_call x1, Pallas kernels, per_device(): pl.pallas_call(interp_kernel, grid=(SIGMA // per_step,), in_specs=[whole(...  7.46 us
    unnamed x25, local copies, waits for them, and re-layouts  6.79 us
    all_to_all x1, starting transfers between devices, per_device(): lax.all_to_all(sigma_blocks.reshape(lon_count, CAP * 2 * SIGMA_PAD, 128),...  6.41 us
  transfers between devices with their start and end apart: 9, of which 6 were waited for; matrix products, arithmetic and copies ran while one was open for 2% of the time, Pallas kernels for 20%

profile of v3, /device:TPU:13, one launch (start us, length us, event | category | flops | bytes accessed | tf_op | source)
XLA Modules:
  0.0 105.2 jit_solution(14355147831257343268)
XLA Ops:
  0.6 1.8 %copy-done = f32[75,24,384]{2,1,0:T(8,128)S(1)} copy-done((f32[75,24,384]{2,1,0:T(8,128)S(1)}, f32[75,24,384]{2,1,0:T(8,128)}, u32[]{:S(2)}) %copy-start) | copy-done | bytes 2764824
  2.4 5.4 %pack_edges.1 = (f32[240,384]{1,0:T(8,128)S(1)}, f32[240,384]{1,0:T(8,128)S(1)}, f32[3,24,128]{2,1,0:T(8,128)S(1)}, f32[3,24,128]{2,1,0:T(8,128)S(1)}) custom-call(f32[75,24,384]{2,1,0:T(8,128)S(1)} %copy-done, f32[75,24,384]{2,1,0:T(8,128)} %v_ref.5, f32[75,24,384]{2,1,0:T(8,128)} %t_ref.5), custom_call_target="tpu_custom_call" | custom-call | tf_op jit(solution)/shard_map/pack_edges/pallas_call | solution.py:280
  7.8 3.1 %collective-permute-start.2 = (f32[240,384]{1,0:T(8,128)S(1)}, f32[240,384]{1,0:T(8,128)S(1)}, u32[]{:S(2)}, u32[]{:S(2)}) collective-permute-start(f32[240,384]{1,0:T(8,128)S(1)} %get-tuple-element.18), channel_id=1, source_target_pairs={{1,0},{2,1},{3,2},{5,4},{6,5},{7,6},{9,8},{10,9},{11,10},{13,12},{... | collective-permute-start | bytes 1105928 | tf_op jit(solution)/shard_map/ppermute | solution.py:266
  10.9 2.2 %collective-permute-start.3 = (f32[240,384]{1,0:T(8,128)S(1)}, f32[240,384]{1,0:T(8,128)S(1)}, u32[]{:S(2)}, u32[]{:S(2)}) collective-permute-start(f32[240,384]{1,0:T(8,128)S(1)} %get-tuple-element.19), channel_id=1, source_target_pairs={{0,1},{1,2},{2,3},{4,5},{5,6},{6,7},{8,9},{9,10},{10,11},{12,13},{... | collective-permute-start | bytes 1105928 | tf_op jit(solution)/shard_map/ppermute | solution.py:266
  13.1 1.3 %collective-permute-start = (f32[3,24,128]{2,1,0:T(8,128)S(1)}, f32[3,24,128]{2,1,0:T(8,128)S(1)}, u32[]{:S(2)}, u32[]{:S(2)}) collective-permute-start(f32[3,24,128]{2,1,0:T(8,128)S(1)} %get-tuple-element.16), channel_id=1, source_target_pairs={{4,0},{8,4},{12,8},{16,12},{20,16},{24,20},{28,24},{0,28},{5,1},{9... | collective-permute-start | bytes 110600 | tf_op jit(solution)/shard_map/ppermute | solution.py:266
  14.4 1.2 %collective-permute-start.1 = (f32[3,24,128]{2,1,0:T(8,128)S(1)}, f32[3,24,128]{2,1,0:T(8,128)S(1)}, u32[]{:S(2)}, u32[]{:S(2)}) collective-permute-start(f32[3,24,128]{2,1,0:T(8,128)S(1)} %get-tuple-element.17), channel_id=1, source_target_pairs={{0,4},{4,8},{8,12},{12,16},{16,20},{20,24},{24,28},{28,0},{1,5},{5... | collective-permute-start | bytes 110600 | tf_op jit(solution)/shard_map/ppermute | solution.py:266
  17.5 1.6 %collective-permute-done.2.north_ref = f32[240,384]{1,0:T(8,128)S(1)} collective-permute-done((f32[240,384]{1,0:T(8,128)S(1)}, f32[240,384]{1,0:T(8,128)S(1)}, u32[]{:S(2)}, u32[]{:S(2)}) %collective-permute-start.2) | collective-permute-done | bytes 368672 | tf_op jit(solution)/shard_map/ppermute | solution.py:266
  19.1 7.8 %collective-permute-done.3.south_ref = f32[240,384]{1,0:T(8,128)S(1)} collective-permute-done((f32[240,384]{1,0:T(8,128)S(1)}, f32[240,384]{1,0:T(8,128)S(1)}, u32[]{:S(2)}, u32[]{:S(2)}) %collective-permute-start.3) | collective-permute-done | bytes 368672 | tf_op jit(solution)/shard_map/ppermute | solution.py:266
  27.0 9.7 %tracer_step.1 = (f32[75,24,384]{2,1,0:T(8,128)}, f32[3,1800,128]{2,1,0:T(8,128)S(1)}, f32[160,384]{1,0:T(8,128)S(1)}, f32[160,384]{1,0:T(8,128)S(1)}, f32[80,128]{1,0:T(8,128)S(1)}, /*index=5*/f32[80,128]{1,0:T(8,128)S(1)}) custom-call(f32[75,24,384]{2,1,0:T(8,128)} %u_ref.5, f32[75,24,384]{2,1,0:T(8,128)} %v_ref.5, f32[75,24,384]{2,1,0:T(8,128)} %t_ref.5, ...), custom_call_target="tpu_custom_call" | custom-call | tf_op jit(solution)/shard_map/tracer_step/pallas_call | solution.py:299
  36.7 1.6 %collective-permute-start.4 = (f32[80,128]{1,0:T(8,128)S(1)}, f32[80,128]{1,0:T(8,128)S(1)}, u32[]{:S(2)}, u32[]{:S(2)}) collective-permute-start(f32[80,128]{1,0:T(8,128)S(1)} %get-tuple-element.24), channel_id=1, source_target_pairs={{4,0},{8,4},{12,8},{16,12},{20,16},{24,20},{28,24},{0,28},{5,1},{9... | collective-permute-start | bytes 122888 | tf_op jit(solution)/shard_map/ppermute | solution.py:266
  38.5 1.2 %collective-permute-start.5 = (f32[80,128]{1,0:T(8,128)S(1)}, f32[80,128]{1,0:T(8,128)S(1)}, u32[]{:S(2)}, u32[]{:S(2)}) collective-permute-start(f32[80,128]{1,0:T(8,128)S(1)} %get-tuple-element.25), channel_id=1, source_target_pairs={{0,4},{4,8},{8,12},{12,16},{16,20},{20,24},{24,28},{28,0},{1,5},{5... | collective-permute-start | bytes 122888 | tf_op jit(solution)/shard_map/ppermute | solution.py:266
  39.7 1.8 %collective-permute-done.4.east_ref = f32[80,128]{1,0:T(8,128)S(1)} collective-permute-done((f32[80,128]{1,0:T(8,128)S(1)}, f32[80,128]{1,0:T(8,128)S(1)}, u32[]{:S(2)}, u32[]{:S(2)}) %collective-permute-start.4) | collective-permute-done | bytes 40992 | tf_op jit(solution)/shard_map/ppermute | solution.py:266
  41.6 1.9 %collective-permute-start.6 = (f32[160,512]{1,0:T(8,128)S(1)}, f32[160,512]{1,0:T(8,128)S(1)}, u32[]{:S(2)}, u32[]{:S(2)}) collective-permute-start(f32[160,512]{1,0:T(8,128)S(1)} %get-tuple-element.29), channel_id=1, source_target_pairs={{1,0},{2,1},{3,2},{5,4},{6,5},{7,6},{9,8},{10,9},{11,10},{13,12},{... | collective-permute-start | bytes 983048 | tf_op jit(solution)/shard_map/ppermute | solution.py:266
  43.5 3.4 %collective-permute-start.7 = (f32[160,512]{1,0:T(8,128)S(1)}, f32[160,512]{1,0:T(8,128)S(1)}, u32[]{:S(2)}, u32[]{:S(2)}) collective-permute-start(f32[160,512]{1,0:T(8,128)S(1)} %get-tuple-element.28), channel_id=1, source_target_pairs={{0,1},{1,2},{2,3},{4,5},{5,6},{6,7},{8,9},{9,10},{10,11},{12,13},{... | collective-permute-start | bytes 983048 | tf_op jit(solution)/shard_map/ppermute | solution.py:266
  47.2 5.1 %collective-permute-done.6.north_ref = f32[160,512]{1,0:T(8,128)S(1)} collective-permute-done((f32[160,512]{1,0:T(8,128)S(1)}, f32[160,512]{1,0:T(8,128)S(1)}, u32[]{:S(2)}, u32[]{:S(2)}) %collective-permute-start.6) | collective-permute-done | bytes 327712 | tf_op jit(solution)/shard_map/ppermute | solution.py:266
  52.3 5.2 %collective-permute-done.7.south_ref = f32[160,512]{1,0:T(8,128)S(1)} collective-permute-done((f32[160,512]{1,0:T(8,128)S(1)}, f32[160,512]{1,0:T(8,128)S(1)}, u32[]{:S(2)}, u32[]{:S(2)}) %collective-permute-start.7) | collective-permute-done | bytes 327712 | tf_op jit(solution)/shard_map/ppermute | solution.py:266
  57.5 7.9 %sigma_rims.1 = f32[16,2,32,128]{3,2,1,0:T(8,128)S(1)} custom-call(s32[16]{0:T(128)S(1)} %select_reduce_fusion.block_ref, f32[3,1800,128]{2,1,0:T(8,128)S(1)} %get-tuple-element.23.x_ref, f32[80,128]{1,0:T(8,128)S(1)} %collective-permute-done.4.east_ref, f32[80,128]{1,0:T(8,128)S(1)} %collective-permute-done.5.west_ref, ...), custom_call_target="tpu_custom_call" | custom-call | tf_op jit(solution)/shard_map/sigma_rims/pallas_call | solution.py:346
  66.2 6.4 %all-to-all-start = ((f32[8,128,128]{2,1,0:T(8,128)}), f32[8,128,128]{2,1,0:T(8,128)S(1)}, u32[]{:S(2)}, u32[]{:S(2)}) async-start(f32[8,128,128]{2,1,0:T(8,128)} %bitcast.12), calls=%async_computation | async-start | bytes 1048576 | tf_op jit(solution)/shard_map/all_to_all | solution.py:361
  72.7 1.0 copy-done.4
  73.7 1.0 copy-done.6
  74.7 20.9 %momentum_step.1 = (f32[75,24,384]{2,1,0:T(8,128)}, f32[75,24,384]{2,1,0:T(8,128)}) custom-call(f32[75,24,384]{2,1,0:T(8,128)S(1)} %copy-done.1, f32[75,24,384]{2,1,0:T(8,128)} %v_ref.5, f32[75,24,384]{2,1,0:T(8,128)} %t_ref.5, s32[24,384]{1,0:T(8,128)S(1)} %copy-done.9, f32[24,384]{1,0:T(8,128)S(1)} %broadcast_in_dim.6.coriolis_ref, ...), custom_call_target="tpu_custom_call" | custom-call | flops 41472000 | bytes 13824000 | tf_op jit(solution)/shard_map/momentum_step/pallas_call | solution.py:318
  95.6 1.1 %copy-done.7 = bf16[256,1296]{1,0:T(8,128)(2,1)S(1)} copy-done((bf16[256,1296]{1,0:T(8,128)(2,1)S(1)}, bf16[256,1296]{1,0:T(8,128)(2,1)}, u32[]{:S(2)}) %copy-start.7) | copy-done | bytes 663576
  96.7 1.1 %copy-done.8 = bf16[256,1296]{1,0:T(8,128)(2,1)S(1)} copy-done((bf16[256,1296]{1,0:T(8,128)(2,1)S(1)}, bf16[256,1296]{1,0:T(8,128)(2,1)}, u32[]{:S(2)}) %copy-start.8) | copy-done | bytes 663576
  97.8 7.5 %interpolate.1 = f32[480,1296]{1,0:T(8,128)} custom-call(f32[1024,128]{1,0:T(8,128)S(1)} %bitcast.11, bf16[256,1296]{1,0:T(8,128)(2,1)S(1)} %copy-done.7, bf16[256,1296]{1,0:T(8,128)(2,1)S(1)} %copy-done.8), custom_call_target="tpu_custom_call" | custom-call | tf_op jit(solution)/shard_map/interpolate/pallas_call | solution.py:370
  (40 shorter events, 3.3 us)
Async XLA Ops:
  0.6 1.8 %copy-start = (f32[75,24,384]{2,1,0:T(8,128)S(1)}, f32[75,24,384]{2,1,0:T(8,128)}, u32[]{:S(2)}) copy-start(f32[75,24,384]{2,1,0:T(8,128)} %u_ref.5) | copy-start | bytes 8294404
  2.4 13.2 %copy-start.11 = (s32[2,32]{1,0:T(2,128)S(1)}, s32[2,32]{1,0:T(2,128)}, u32[]{:S(2)}) copy-start(s32[2,32]{1,0:T(2,128)} %param.12) | copy-start | bytes 772
  2.4 13.5 %copy-start.10 = (s32[2,32,31]{1,0,2:T(2,128)S(1)}, s32[2,32,31]{1,0,2:T(2,128)}, u32[]{:S(2)}) copy-start(s32[2,32,31]{1,0,2:T(2,128)} %param.11) | copy-start | bytes 23812
  2.4 24.6 %copy-start.9 = (s32[24,384]{1,0:T(8,128)S(1)}, s32[24,384]{1,0:T(8,128)}, u32[]{:S(2)}) copy-start(s32[24,384]{1,0:T(8,128)} %mask_ref.3) | copy-start | bytes 110596
  7.8 11.3 %collective-permute-start.2 = (f32[240,384]{1,0:T(8,128)S(1)}, f32[240,384]{1,0:T(8,128)S(1)}, u32[]{:S(2)}, u32[]{:S(2)}) collective-permute-start(f32[240,384]{1,0:T(8,128)S(1)} %get-tuple-element.18), channel_id=1, source_target_pairs={{1,0},{2,1},{3,2},{5,4},{6,5},{7,6},{9,8},{10,9},{11,10},{13,12},{... | collective-permute-start | bytes 1105928 | tf_op jit(solution)/shard_map/ppermute | solution.py:266
  10.9 16.1 %collective-permute-start.3 = (f32[240,384]{1,0:T(8,128)S(1)}, f32[240,384]{1,0:T(8,128)S(1)}, u32[]{:S(2)}, u32[]{:S(2)}) collective-permute-start(f32[240,384]{1,0:T(8,128)S(1)} %get-tuple-element.19), channel_id=1, source_target_pairs={{0,1},{1,2},{2,3},{4,5},{5,6},{6,7},{8,9},{9,10},{10,11},{12,13},{... | collective-permute-start | bytes 1105928 | tf_op jit(solution)/shard_map/ppermute | solution.py:266
  13.1 4.4 %collective-permute-start = (f32[3,24,128]{2,1,0:T(8,128)S(1)}, f32[3,24,128]{2,1,0:T(8,128)S(1)}, u32[]{:S(2)}, u32[]{:S(2)}) collective-permute-start(f32[3,24,128]{2,1,0:T(8,128)S(1)} %get-tuple-element.16), channel_id=1, source_target_pairs={{4,0},{8,4},{12,8},{16,12},{20,16},{24,20},{28,24},{0,28},{5,1},{9... | collective-permute-start | bytes 110600 | tf_op jit(solution)/shard_map/ppermute | solution.py:266
  14.4 3.1 %collective-permute-start.1 = (f32[3,24,128]{2,1,0:T(8,128)S(1)}, f32[3,24,128]{2,1,0:T(8,128)S(1)}, u32[]{:S(2)}, u32[]{:S(2)}) collective-permute-start(f32[3,24,128]{2,1,0:T(8,128)S(1)} %get-tuple-element.17), channel_id=1, source_target_pairs={{0,4},{4,8},{8,12},{12,16},{16,20},{20,24},{24,28},{28,0},{1,5},{5... | collective-permute-start | bytes 110600 | tf_op jit(solution)/shard_map/ppermute | solution.py:266
  19.1 17.6 %copy-start.3 = (f32[240,384]{1,0:T(8,128)}, f32[240,384]{1,0:T(8,128)S(1)}, u32[]{:S(2)}) copy-start(f32[240,384]{1,0:T(8,128)S(1)} %collective-permute-done.2.north_ref) | copy-start | bytes 1105924
  27.0 9.7 %copy-start.5 = (f32[240,384]{1,0:T(8,128)}, f32[240,384]{1,0:T(8,128)S(1)}, u32[]{:S(2)}) copy-start(f32[240,384]{1,0:T(8,128)S(1)} %collective-permute-done.3.south_ref) | copy-start | bytes 1105924
  36.7 4.8 %collective-permute-start.4 = (f32[80,128]{1,0:T(8,128)S(1)}, f32[80,128]{1,0:T(8,128)S(1)}, u32[]{:S(2)}, u32[]{:S(2)}) collective-permute-start(f32[80,128]{1,0:T(8,128)S(1)} %get-tuple-element.24), channel_id=1, source_target_pairs={{4,0},{8,4},{12,8},{16,12},{20,16},{24,20},{28,24},{0,28},{5,1},{9... | collective-permute-start | bytes 122888 | tf_op jit(solution)/shard_map/ppermute | solution.py:266
  38.5 3.0 %collective-permute-start.5 = (f32[80,128]{1,0:T(8,128)S(1)}, f32[80,128]{1,0:T(8,128)S(1)}, u32[]{:S(2)}, u32[]{:S(2)}) collective-permute-start(f32[80,128]{1,0:T(8,128)S(1)} %get-tuple-element.25), channel_id=1, source_target_pairs={{0,4},{4,8},{8,12},{12,16},{16,20},{20,24},{24,28},{28,0},{1,5},{5... | collective-permute-start | bytes 122888 | tf_op jit(solution)/shard_map/ppermute | solution.py:266
  41.6 10.8 %collective-permute-start.6 = (f32[160,512]{1,0:T(8,128)S(1)}, f32[160,512]{1,0:T(8,128)S(1)}, u32[]{:S(2)}, u32[]{:S(2)}) collective-permute-start(f32[160,512]{1,0:T(8,128)S(1)} %get-tuple-element.29), channel_id=1, source_target_pairs={{1,0},{2,1},{3,2},{5,4},{6,5},{7,6},{9,8},{10,9},{11,10},{13,12},{... | collective-permute-start | bytes 983048 | tf_op jit(solution)/shard_map/ppermute | solution.py:266
  43.5 14.0 %collective-permute-start.7 = (f32[160,512]{1,0:T(8,128)S(1)}, f32[160,512]{1,0:T(8,128)S(1)}, u32[]{:S(2)}, u32[]{:S(2)}) collective-permute-start(f32[160,512]{1,0:T(8,128)S(1)} %get-tuple-element.28), channel_id=1, source_target_pairs={{0,1},{1,2},{2,3},{4,5},{5,6},{6,7},{8,9},{9,10},{10,11},{12,13},{... | collective-permute-start | bytes 983048 | tf_op jit(solution)/shard_map/ppermute | solution.py:266
  47.0 25.7 %copy-start.1 = (f32[75,24,384]{2,1,0:T(8,128)S(1)}, f32[75,24,384]{2,1,0:T(8,128)}, u32[]{:S(2)}) copy-start(f32[75,24,384]{2,1,0:T(8,128)} %u_ref.5) | copy-start | bytes 8294404
  65.4 0.8 copy-start.2
  66.2 29.4 %all-to-all-start = ((f32[8,128,128]{2,1,0:T(8,128)}), f32[8,128,128]{2,1,0:T(8,128)S(1)}, u32[]{:S(2)}, u32[]{:S(2)}) async-start(f32[8,128,128]{2,1,0:T(8,128)} %bitcast.12), calls=%async_computation | async-start | bytes 1048576 | tf_op jit(solution)/shard_map/all_to_all | solution.py:361
  72.7 1.0 copy-start.4
  73.7 1.0 copy-start.6
  95.6 1.1 %copy-start.7 = (bf16[256,1296]{1,0:T(8,128)(2,1)S(1)}, bf16[256,1296]{1,0:T(8,128)(2,1)}, u32[]{:S(2)}) copy-start(bf16[256,1296]{1,0:T(8,128)(2,1)} %constant.30.high_ref) | copy-start | bytes 1990660
  96.7 1.1 %copy-start.8 = (bf16[256,1296]{1,0:T(8,128)(2,1)S(1)}, bf16[256,1296]{1,0:T(8,128)(2,1)}, u32[]{:S(2)}) copy-start(bf16[256,1296]{1,0:T(8,128)(2,1)} %constant.33.low_ref) | copy-start | bytes 1990660
